TPU v7x, 256 devices: a whole 4x4x8 slice. The times are simulated.
256 devices in a mesh: grp: 16 (over z, x_hi), sp: 16 (over x_lo, y, core).
Axes of the slice: x: 4 (x_hi: 2, x_lo: 2; x = x_hi * 2 + x_lo), y: 4, z: 8, core: 2. Of those that a mesh axis runs over, the one named last changes fastest.
Arguments:
- queries: bfloat16 [16, 3072, 2048], P('grp', 'sp'), may hold values from -15 to 15
- keys: bfloat16 [16, 3072, 2048], P('grp', 'sp'), may hold values from -6 to 6
- values: bfloat16 [16, 3072, 2048], P('grp', 'sp'), may hold values from -6 to 6
- ref_cache: bfloat16 [16, 2, 2048, 2048], P('grp', None, 'sp'), may hold values from -6 to 6
- ref_ids: int32 [16], replicated, may hold values from 0 to 15
- ref_owner: int32 [16], replicated, may hold values from 0 to 15, each once
- ref_lens: int32 [16], replicated, may hold values from 256 to 2048, as said below
Outputs:
- attended: bfloat16 [16, 3072, 2048], P('grp', 'sp')
Inputs may be any that keep to these rules, and one draw needn't show every extreme that they name: `ref_owner`: each reference image lies in exactly one cache row. `ref_lens`: some reference has 2048 live tokens and some 2048 // 8.
All inputs are finite; a program needn't handle non-finite values.
Results may differ from a plain program's by a relative error of at most 0.0031.
Values may be sent and summed in bfloat16 or wider, within the bound.
No kernel may reach another device: no remote copies, remote signals or barrier semaphores. Data moves between devices by JAX's collectives and lax.ppermute only.
A program may use at most 64 MiB of HBM per device.

v0:
```python
import math

import jax
import jax.numpy as jnp
from jax import lax
from jax.sharding import PartitionSpec as P

HEAD_DIM = 128


def attend(own_q, own_k, own_v, ref_pair, live_len):
    tokens, feat_width = own_q.shape
    head_count = feat_width // HEAD_DIM
    key_set = jnp.concatenate([own_k, ref_pair[0]], axis=0)
    value_set = jnp.concatenate([own_v, ref_pair[1]], axis=0)
    total_keys = key_set.shape[0]
    key_heads = key_set.reshape(total_keys, head_count, HEAD_DIM)
    value_heads = value_set.reshape(total_keys, head_count, HEAD_DIM)
    live_mask = jnp.arange(total_keys, dtype=jnp.int32) < tokens + live_len
    block_rows = math.gcd(tokens, 512)
    query_blocks = own_q.reshape(tokens // block_rows, block_rows, head_count, HEAD_DIM)
    score_scale = HEAD_DIM ** (-0.5)

    def one_block(query_rows):
        scores = (
            jnp.einsum("qhd,khd->hqk", query_rows, key_heads, preferred_element_type=jnp.float32)
            * score_scale
        )
        scores = jnp.where(live_mask[None, None, :], scores, -jnp.inf)
        row_peak = jnp.max(scores, axis=-1, keepdims=True)
        weights = jnp.exp(scores - row_peak)
        row_total = jnp.sum(weights, axis=-1, keepdims=True)
        soft_probs = weights.astype(jnp.bfloat16)
        mixed_out = jnp.einsum(
            "hqk,khd->qhd", soft_probs, value_heads, preferred_element_type=jnp.float32
        )
        scaled = mixed_out / jnp.transpose(row_total, (1, 0, 2))
        return scaled.astype(jnp.bfloat16).reshape(block_rows, feat_width)

    return lax.map(one_block, query_blocks).reshape(tokens, feat_width)


def row_picker(wanted, carry, piece):
    inside = jnp.logical_and(wanted >= 0, wanted < piece.shape[0])
    picked = lax.dynamic_index_in_dim(
        piece, jnp.clip(wanted, 0, piece.shape[0] - 1), 0, keepdims=False
    )
    return jnp.where(inside, picked, carry)


def shards(queries, keys, values, ref_cache, ref_ids, ref_owner, ref_lens):
    my_group = lax.axis_index("grp")
    wanted_ref = ref_ids[my_group]
    need_row = ref_owner[wanted_ref]
    need_len = ref_lens[wanted_ref]
    own_q, own_k, own_v = (
        lax.all_to_all(queries[0], "sp", split_axis=1, concat_axis=0, tiled=True),
        lax.all_to_all(keys[0], "sp", split_axis=1, concat_axis=0, tiled=True),
        lax.all_to_all(values[0], "sp", split_axis=1, concat_axis=0, tiled=True),
    )
    cache_slot = ref_cache[0]
    empty_slot = jnp.zeros_like(cache_slot)
    my_slot = row_picker(
        need_row, empty_slot, lax.all_gather(cache_slot[None], "grp", axis=0, tiled=True)
    )
    my_slot = lax.all_to_all(my_slot, "sp", split_axis=2, concat_axis=1, tiled=True)
    head_result = attend(own_q, own_k, own_v, my_slot, need_len)
    returned = lax.all_to_all(head_result, "sp", split_axis=0, concat_axis=1, tiled=True)
    return returned[None]


def solution(mesh):
    in_specs = (
        P("grp", "sp", None),
        P("grp", "sp", None),
        P("grp", "sp", None),
        P("grp", None, "sp", None),
        P(),
        P(),
        P(),
    )
    out_specs = P("grp", "sp", None)
    return jax.shard_map(shards, mesh=mesh, in_specs=in_specs, out_specs=out_specs, check_vma=False)
```

profile of v0, /device:TPU:1, one launch (start us, length us, event | category | flops | bytes accessed | tf_op | source)
XLA Modules:
  0.0 371.3 jit_solution(13761455336722245959)
XLA Ops:
  9.6 6.9 %all-to-all-start.1 = ((bf16[192,16,128]{2,0,1:T(8,128)(2,1)}), bf16[192,16,128]{2,0,1:T(8,128)(2,1)S(1)}, u32[]{:S(2)}, u32[]{:S(2)}) async-start(bf16[192,16,128]{2,0,1:T(8,128)(2,1)} %copy.31), calls=%async_computation.1 | async-start | bytes 1572864 | tf_op jit(solution)/shard_map/all_to_all | solution.py:58
  19.7 1.3 dynamic_slice.19
  22.9 215.5 %all-gather.2.cloned.1.call-done = bf16[16,2,128,2048]{3,2,1,0:T(8,128)(2,1)} async-done(((bf16[1,2,128,2048]{3,2,1,0:T(8,128)(2,1)}), bf16[16,2,128,2048]{3,2,1,0:T(8,128)(2,1)}) %all-gather.2.cloned.1.call-update) | async-done | bytes 16777232 | tf_op jit(solution)/shard_map/all_gather | solution.py:64
  238.4 1.3 select_bitcast_fusion
  239.7 2.0 copy.32
  241.8 5.4 %all-to-all-start.2 = ((bf16[2,128,2048]{1,0,2:T(2,128)(2,1)}), bf16[2,128,2048]{1,0,2:T(2,128)(2,1)S(1)}, u32[]{:S(2)}, u32[]{:S(2)}) async-start(bf16[2,128,2048]{1,0,2:T(2,128)(2,1)} %copy.32), calls=%async_computation.2 | async-start | bytes 2097152 | tf_op jit(solution)/shard_map/all_to_all | solution.py:66
  248.5 14.6 %all-to-all-done.2 = bf16[2,128,2048]{1,0,2:T(2,128)(2,1)S(1)} async-done(((bf16[2,128,2048]{1,0,2:T(2,128)(2,1)}), bf16[2,128,2048]{1,0,2:T(2,128)(2,1)S(1)}, u32[]{:S(2)}, u32[]{:S(2)}) %all-to-all-start.2) | async-done | bytes 1048608 | tf_op jit(solution)/shard_map/all_to_all | solution.py:66
  263.0 4.9 %all-to-all-start.3 = ((bf16[192,16,128]{2,0,1:T(8,128)(2,1)}), bf16[192,16,128]{2,0,1:T(8,128)(2,1)}, u32[]{:S(2)}, u32[]{:S(2)}) async-start(bf16[192,16,128]{2,0,1:T(8,128)(2,1)} %copy.34), calls=%async_computation.3 | async-start | bytes 1572864 | tf_op jit(solution)/shard_map/all_to_all | solution.py:59
  272.1 8.9 %all-to-all-done.3 = bf16[192,16,128]{2,0,1:T(8,128)(2,1)} async-done(((bf16[192,16,128]{2,0,1:T(8,128)(2,1)}), bf16[192,16,128]{2,0,1:T(8,128)(2,1)}, u32[]{:S(2)}, u32[]{:S(2)}) %all-to-all-start.3) | async-done | bytes 786464 | tf_op jit(solution)/shard_map/all_to_all | solution.py:59
  281.1 4.3 %all-to-all-start = ((bf16[192,16,128]{2,0,1:T(8,128)(2,1)}), bf16[192,16,128]{2,0,1:T(8,128)(2,1)S(1)}, u32[]{:S(2)}, u32[]{:S(2)}) async-start(bf16[192,16,128]{2,0,1:T(8,128)(2,1)} %copy.30), calls=%async_computation | async-start | bytes 1572864 | tf_op jit(solution)/shard_map/all_to_all | solution.py:57
  286.5 2.3 maximum_bitcast_fusion.1
  288.8 9.6 %all-to-all-done = bf16[192,16,128]{2,0,1:T(8,128)(2,1)S(1)} async-done(((bf16[192,16,128]{2,0,1:T(8,128)(2,1)}), bf16[192,16,128]{2,0,1:T(8,128)(2,1)S(1)}, u32[]{:S(2)}, u32[]{:S(2)}) %all-to-all-start) | async-done | bytes 786464 | tf_op jit(solution)/shard_map/all_to_all | solution.py:57
  298.4 47.2 %while.11 = (s32[]{:T(128)}, bf16[6,512,128]{2,1,0:T(8,128)(2,1)}, bf16[6,512,1,128]{3,1,2,0:T(8,128)(2,1)S(1)}, bf16[5120,1,128]{2,0,1:T(8,128)(2,1)S(1)}, bf16...) while((s32[]{:T(128)}, bf16[6,512,128]{2,1,0:T(8,128)(2,1)}, ...), condition=%wide.region_3.4_spmd.clone, body=%wide.region_0.3_spmd.clone.sunk | while | flops 1371148288 | bytes 39614588 | solution.py:40
  298.4 1.7 fusion.49
  300.2 2.4 fusion.50
  302.6 3.7 %fusion.51 = bf16[6,512,128]{2,1,0:T(8,128)(2,1)} fusion(bf16[6,512,128]{2,1,0:T(8,128)(2,1)} %get-tuple-element.142, s32[]{:T(128)S(6)} %copy.43, bf16[5120,1,128]{2,0,1:T(8,128)(2,1)S(1)} %copy-done, f32[512,5120]{1,0:T(8,128)S(1)} %get-tuple-element.132, f32[512]{0:T(512)S(1)} %get-tuple-element.133, pred[5120]{0:T(1024)(128)(4,1)S(1)} %iota_compare_fusion.2, ...), kind=kOutput, calls=%fused_computation.15.clone.1 | convolution fusion | flops 681705472 | bytes 11936772 | tf_op jit(solution)/shard_map/while/body/eval_jaxpr/hqk,khd->qhd/dot_general | solution.py:34
  306.3 1.7 fusion.49
  308.0 2.4 fusion.50
  310.4 3.7 %fusion.51 = bf16[6,512,128]{2,1,0:T(8,128)(2,1)} fusion(bf16[6,512,128]{2,1,0:T(8,128)(2,1)} %get-tuple-element.142, s32[]{:T(128)S(6)} %copy.43, bf16[5120,1,128]{2,0,1:T(8,128)(2,1)S(1)} %copy-done, f32[512,5120]{1,0:T(8,128)S(1)} %get-tuple-element.132, f32[512]{0:T(512)S(1)} %get-tuple-element.133, pred[5120]{0:T(1024)(128)(4,1)S(1)} %iota_compare_fusion.2, ...), kind=kOutput, calls=%fused_computation.15.clone.1 | convolution fusion | flops 681705472 | bytes 11936772 | tf_op jit(solution)/shard_map/while/body/eval_jaxpr/hqk,khd->qhd/dot_general | solution.py:34
  314.2 1.7 fusion.49
  315.9 2.4 fusion.50
  318.3 3.7 %fusion.51 = bf16[6,512,128]{2,1,0:T(8,128)(2,1)} fusion(bf16[6,512,128]{2,1,0:T(8,128)(2,1)} %get-tuple-element.142, s32[]{:T(128)S(6)} %copy.43, bf16[5120,1,128]{2,0,1:T(8,128)(2,1)S(1)} %copy-done, f32[512,5120]{1,0:T(8,128)S(1)} %get-tuple-element.132, f32[512]{0:T(512)S(1)} %get-tuple-element.133, pred[5120]{0:T(1024)(128)(4,1)S(1)} %iota_compare_fusion.2, ...), kind=kOutput, calls=%fused_computation.15.clone.1 | convolution fusion | flops 681705472 | bytes 11936772 | tf_op jit(solution)/shard_map/while/body/eval_jaxpr/hqk,khd->qhd/dot_general | solution.py:34
  322.0 1.7 fusion.49
  323.8 2.4 fusion.50
  326.1 3.7 %fusion.51 = bf16[6,512,128]{2,1,0:T(8,128)(2,1)} fusion(bf16[6,512,128]{2,1,0:T(8,128)(2,1)} %get-tuple-element.142, s32[]{:T(128)S(6)} %copy.43, bf16[5120,1,128]{2,0,1:T(8,128)(2,1)S(1)} %copy-done, f32[512,5120]{1,0:T(8,128)S(1)} %get-tuple-element.132, f32[512]{0:T(512)S(1)} %get-tuple-element.133, pred[5120]{0:T(1024)(128)(4,1)S(1)} %iota_compare_fusion.2, ...), kind=kOutput, calls=%fused_computation.15.clone.1 | convolution fusion | flops 681705472 | bytes 11936772 | tf_op jit(solution)/shard_map/while/body/eval_jaxpr/hqk,khd->qhd/dot_general | solution.py:34
  329.9 1.7 fusion.49
  331.6 2.4 fusion.50
  334.0 3.7 %fusion.51 = bf16[6,512,128]{2,1,0:T(8,128)(2,1)} fusion(bf16[6,512,128]{2,1,0:T(8,128)(2,1)} %get-tuple-element.142, s32[]{:T(128)S(6)} %copy.43, bf16[5120,1,128]{2,0,1:T(8,128)(2,1)S(1)} %copy-done, f32[512,5120]{1,0:T(8,128)S(1)} %get-tuple-element.132, f32[512]{0:T(512)S(1)} %get-tuple-element.133, pred[5120]{0:T(1024)(128)(4,1)S(1)} %iota_compare_fusion.2, ...), kind=kOutput, calls=%fused_computation.15.clone.1 | convolution fusion | flops 681705472 | bytes 11936772 | tf_op jit(solution)/shard_map/while/body/eval_jaxpr/hqk,khd->qhd/dot_general | solution.py:34
  337.7 1.7 fusion.49
  339.5 2.4 fusion.50
  341.9 3.7 %fusion.51 = bf16[6,512,128]{2,1,0:T(8,128)(2,1)} fusion(bf16[6,512,128]{2,1,0:T(8,128)(2,1)} %get-tuple-element.142, s32[]{:T(128)S(6)} %copy.43, bf16[5120,1,128]{2,0,1:T(8,128)(2,1)S(1)} %copy-done, f32[512,5120]{1,0:T(8,128)S(1)} %get-tuple-element.132, f32[512]{0:T(512)S(1)} %get-tuple-element.133, pred[5120]{0:T(1024)(128)(4,1)S(1)} %iota_compare_fusion.2, ...), kind=kOutput, calls=%fused_computation.15.clone.1 | convolution fusion | flops 681705472 | bytes 11936772 | tf_op jit(solution)/shard_map/while/body/eval_jaxpr/hqk,khd->qhd/dot_general | solution.py:34
  345.6 17.1 %all_to_all.85 = bf16[16,192,128]{2,1,0:T(8,128)(2,1)S(1)} all-to-all(bf16[16,192,128]{2,1,0:T(8,128)(2,1)} %bitcast.100), channel_id=1, replica_groups=mesh['grp'=16,'sp'=16] {'sp'}, dimensions={0} | all-to-all | bytes 1572864 | tf_op jit(solution)/shard_map/all_to_all | solution.py:68
  (41 shorter events, 12.2 us)
Async XLA Ops:
  6.5 240.6 %copy-start.1 = (bf16[1,192,2048]{2,1,0:T(8,128)(2,1)S(1)}, bf16[1,192,2048]{2,1,0:T(8,128)(2,1)}, u32[]{:S(2)}) copy-start(bf16[1,192,2048]{2,1,0:T(8,128)(2,1)} %param.11) | copy-start | bytes 2359300
  6.5 261.4 %copy-start.3 = (s32[16]{0:T(128)S(1)}, s32[16]{0:T(128)}, u32[]{:S(2)}) copy-start(s32[16]{0:T(128)} %param.15) | copy-start | bytes 196
  6.5 261.9 %copy-start.2 = (bf16[1,192,2048]{2,1,0:T(8,128)(2,1)S(1)}, bf16[1,192,2048]{2,1,0:T(8,128)(2,1)}, u32[]{:S(2)}) copy-start(bf16[1,192,2048]{2,1,0:T(8,128)(2,1)} %param.9) | copy-start | bytes 2359300
  6.5 231.9 %all-gather.2.cloned.1.call-start = ((), (), s32[]{:S(2)}) async-start(), calls=%async_computation.5 | async-start | bytes 17825792 | tf_op jit(solution)/shard_map/all_gather | solution.py:64
  9.6 232.1 %all-to-all-start.1 = ((bf16[192,16,128]{2,0,1:T(8,128)(2,1)}), bf16[192,16,128]{2,0,1:T(8,128)(2,1)S(1)}, u32[]{:S(2)}, u32[]{:S(2)}) async-start(bf16[192,16,128]{2,0,1:T(8,128)(2,1)} %copy.31), calls=%async_computation.1 | async-start | bytes 1572864 | tf_op jit(solution)/shard_map/all_to_all | solution.py:58
  241.8 21.3 %all-to-all-start.2 = ((bf16[2,128,2048]{1,0,2:T(2,128)(2,1)}), bf16[2,128,2048]{1,0,2:T(2,128)(2,1)S(1)}, u32[]{:S(2)}, u32[]{:S(2)}) async-start(bf16[2,128,2048]{1,0,2:T(2,128)(2,1)} %copy.32), calls=%async_computation.2 | async-start | bytes 2097152 | tf_op jit(solution)/shard_map/all_to_all | solution.py:66
  263.0 18.1 %all-to-all-start.3 = ((bf16[192,16,128]{2,0,1:T(8,128)(2,1)}), bf16[192,16,128]{2,0,1:T(8,128)(2,1)}, u32[]{:S(2)}, u32[]{:S(2)}) async-start(bf16[192,16,128]{2,0,1:T(8,128)(2,1)} %copy.34), calls=%async_computation.3 | async-start | bytes 1572864 | tf_op jit(solution)/shard_map/all_to_all | solution.py:59
  281.1 17.3 %all-to-all-start = ((bf16[192,16,128]{2,0,1:T(8,128)(2,1)}), bf16[192,16,128]{2,0,1:T(8,128)(2,1)S(1)}, u32[]{:S(2)}, u32[]{:S(2)}) async-start(bf16[192,16,128]{2,0,1:T(8,128)(2,1)} %copy.30), calls=%async_computation | async-start | bytes 1572864 | tf_op jit(solution)/shard_map/all_to_all | solution.py:57
  298.4 4.1 %copy-start = (bf16[5120,1,128]{2,0,1:T(8,128)(2,1)S(1)}, bf16[5120,1,128]{2,0,1:T(8,128)(2,1)}, u32[]{:S(2)}) copy-start(bf16[5120,1,128]{2,0,1:T(8,128)(2,1)} %get-tuple-element.152) | copy-start | bytes 3932164 | tf_op jit(solution)/shard_map/while
  306.3 4.1 %copy-start = (bf16[5120,1,128]{2,0,1:T(8,128)(2,1)S(1)}, bf16[5120,1,128]{2,0,1:T(8,128)(2,1)}, u32[]{:S(2)}) copy-start(bf16[5120,1,128]{2,0,1:T(8,128)(2,1)} %get-tuple-element.152) | copy-start | bytes 3932164 | tf_op jit(solution)/shard_map/while
  314.1 4.1 %copy-start = (bf16[5120,1,128]{2,0,1:T(8,128)(2,1)S(1)}, bf16[5120,1,128]{2,0,1:T(8,128)(2,1)}, u32[]{:S(2)}) copy-start(bf16[5120,1,128]{2,0,1:T(8,128)(2,1)} %get-tuple-element.152) | copy-start | bytes 3932164 | tf_op jit(solution)/shard_map/while
  322.0 4.1 %copy-start = (bf16[5120,1,128]{2,0,1:T(8,128)(2,1)S(1)}, bf16[5120,1,128]{2,0,1:T(8,128)(2,1)}, u32[]{:S(2)}) copy-start(bf16[5120,1,128]{2,0,1:T(8,128)(2,1)} %get-tuple-element.152) | copy-start | bytes 3932164 | tf_op jit(solution)/shard_map/while
  329.9 4.1 %copy-start = (bf16[5120,1,128]{2,0,1:T(8,128)(2,1)S(1)}, bf16[5120,1,128]{2,0,1:T(8,128)(2,1)}, u32[]{:S(2)}) copy-start(bf16[5120,1,128]{2,0,1:T(8,128)(2,1)} %get-tuple-element.152) | copy-start | bytes 3932164 | tf_op jit(solution)/shard_map/while
  337.7 4.1 %copy-start = (bf16[5120,1,128]{2,0,1:T(8,128)(2,1)S(1)}, bf16[5120,1,128]{2,0,1:T(8,128)(2,1)}, u32[]{:S(2)}) copy-start(bf16[5120,1,128]{2,0,1:T(8,128)(2,1)} %get-tuple-element.152) | copy-start | bytes 3932164 | tf_op jit(solution)/shard_map/while
Sparse Core Ops, SparseCore 0:
  10.0 228.4 all-gather.1
where the time goes:
time: 372 us; the launch traced here: 371 us
  waiting for transfers between devices  249 us (67%)
  matrix products  32.8 us (9%)
  starting transfers between devices  21.5 us (6%)
  other arithmetic  19.1 us (5%)
  between operations  17.7 us (5%)
  blocking collectives  17.1 us (5%)
  local copies, waits for them, and re-layouts  13.6 us (4%)
    all_gather x1, waiting for transfers between devices, shards(): lax.all_gather(cache_slot[None], 'grp', axis=0, tiled=True)  216 us
    dot_general x6, matrix products, one_block(): jnp.einsum('hqk,khd->qhd', soft_probs, value_heads, preferred_element_typ...  22.3 us
    all_to_all x1, blocking collectives, shards(): lax.all_to_all(head_result, 'sp', split_axis=0, concat_axis=1, tiled=True)  17.1 us
    all_to_all x1, waiting for transfers between devices, shards(): lax.all_to_all(my_slot, 'sp', split_axis=2, concat_axis=1, tiled=True)  14.6 us
    reduce_sum x6, other arithmetic, one_block(): row_total = jnp.sum(weights, axis=-1, keepdims=True)  14.3 us
    dot_general x6, matrix products, one_block(): jnp.einsum('qhd,khd->hqk', query_rows, key_heads, preferred_element_type=...  10.5 us
    all_to_all x1, waiting for transfers between devices, shards(): lax.all_to_all(queries[0], 'sp', split_axis=1, concat_axis=0, tiled=True)  9.63 us
    all_to_all x1, waiting for transfers between devices, shards(): lax.all_to_all(values[0], 'sp', split_axis=1, concat_axis=0, tiled=True)  8.95 us
  transfers between devices with their start and end apart: 5, of which 4 were waited for; matrix products, arithmetic and copies ran while one was open for 4% of the time, Pallas kernels for 0%

commit v1 on v0

v1 whole, which is shorter than its diff:
```python
import functools
import math

import jax
import jax.numpy as jnp
from jax import lax
from jax.experimental import pallas as pl
from jax.experimental.pallas import tpu as pltpu
from jax.sharding import PartitionSpec as P

D = 128
EXP_SCALE = D**-0.5 * math.log2(math.e)
ROWS_CONTRACT = (((1,), (1,)), ((), ()))
VMEM_LIMIT = 48 << 20


def params():
    return pltpu.CompilerParams(vmem_limit_bytes=VMEM_LIMIT)


def whole(memory_space=pltpu.VMEM):
    return pl.BlockSpec(memory_space=memory_space)


def pack_kernel(q_ref, k_ref, v_ref, out_ref):
    for head in range(out_ref.shape[0]):
        cols = slice(head * D, (head + 1) * D)
        for which, ref in enumerate((q_ref, k_ref, v_ref)):
            out_ref[head, which] = ref[:, cols]


def pack_heads(q, k, v):
    tokens, width = q.shape
    heads = width // D
    size = 2 * q.size * q.dtype.itemsize * 3
    return pl.pallas_call(
        pack_kernel,
        in_specs=[whole()] * 3,
        out_specs=whole(),
        out_shape=jax.ShapeDtypeStruct((heads, 3, tokens, D), q.dtype),
        compiler_params=params(),
        cost_estimate=pl.CostEstimate(flops=0, bytes_accessed=size, transcendentals=0),
        name="pack_heads",
    )(q, k, v)


def route_kernel(ids_ref, owner_ref, held_ref, out_ref):
    groups, heads = out_ref.shape[:2]
    for group in range(groups):
        row = owner_ref[ids_ref[group]]
        for head in range(heads):
            out_ref[group, head] = held_ref[row, :, head * D : (head + 1) * D]


def route_pieces(ids, owner, held):
    rows, tokens, width = held.shape
    groups = ids.shape[0]
    heads = width // D
    return pl.pallas_call(
        route_kernel,
        in_specs=[whole(pltpu.SMEM), whole(pltpu.SMEM), whole()],
        out_specs=whole(),
        out_shape=jax.ShapeDtypeStruct((groups, heads, tokens, D), held.dtype),
        compiler_params=params(),
        cost_estimate=pl.CostEstimate(
            flops=0, bytes_accessed=2 * held.size * 2, transcendentals=0
        ),
        name="route_pieces",
    )(ids, owner, held)


def unpack_kernel(x_ref, out_ref):
    for head in range(x_ref.shape[0]):
        out_ref[:, head * D : (head + 1) * D] = x_ref[head]


def unpack_heads(x):
    heads, tokens, _ = x.shape
    return pl.pallas_call(
        unpack_kernel,
        in_specs=[whole()],
        out_specs=whole(),
        out_shape=jax.ShapeDtypeStruct((tokens, heads * D), x.dtype),
        compiler_params=params(),
        name="unpack_heads",
    )(x)


def attend_block(q, k, v_ones, state):
    s = lax.dot_general(q, k, ROWS_CONTRACT, preferred_element_type=jnp.float32)
    peak = jnp.max(s, axis=1, keepdims=True)
    if state is not None:
        peak = jnp.maximum(state[1], peak)
    p = jnp.exp2((s - peak) * EXP_SCALE).astype(jnp.bfloat16)
    part = jnp.dot(p, v_ones, preferred_element_type=jnp.float32)
    if state is not None:
        part = state[0] * jnp.exp2((state[1] - peak) * EXP_SCALE) + part
    return part, peak


def own_kernel(q_ref, k_ref, v_ref, acc_ref, peak_ref, *, rows, sub, steps):
    shards, tokens, _ = k_ref.shape
    per = shards // steps
    q_all = q_ref[...].reshape(rows, D)
    for start in range(0, rows, sub):
        q = q_all[start : start + sub]
        state = None
        for step in range(steps):
            k = k_ref[step * per : (step + 1) * per].reshape(per * tokens, D)
            v = v_ref[step * per : (step + 1) * per].reshape(per * tokens, D)
            v_ones = jnp.concatenate([v, jnp.ones_like(v)], axis=1)
            state = attend_block(q, k, v_ones, state)
        acc_ref[start : start + sub] = state[0]
        peak_ref[start : start + sub] = jnp.broadcast_to(state[1], (sub, D))


def attend_own(qkv):
    shards, _, tokens, _ = qkv.shape
    n = shards * tokens
    rows, sub = 4 * tokens, tokens
    return pl.pallas_call(
        functools.partial(own_kernel, rows=rows, sub=sub, steps=4),
        grid=(n // rows,),
        in_specs=[
            pl.BlockSpec((rows // tokens, None, tokens, D), lambda i: (i, 0, 0, 0)),
            pl.BlockSpec((shards, None, tokens, D), lambda i: (0, 1, 0, 0)),
            pl.BlockSpec((shards, None, tokens, D), lambda i: (0, 2, 0, 0)),
        ],
        out_specs=[
            pl.BlockSpec((rows, 2 * D), lambda i: (i, 0)),
            pl.BlockSpec((rows, D), lambda i: (i, 0)),
        ],
        out_shape=[
            jax.ShapeDtypeStruct((n, 2 * D), jnp.float32),
            jax.ShapeDtypeStruct((n, D), jnp.float32),
        ],
        compiler_params=params(),
        cost_estimate=pl.CostEstimate(
            flops=8 * n * n * D, bytes_accessed=12 * n * D, transcendentals=n * n
        ),
        name="attend_own",
    )(qkv, qkv, qkv)


def ref_kernel(
    live_ref, q_ref, acc_ref, peak_ref, kv_ref, out_ref, k_held, v_held, *, rows, sub, steps
):
    halves, pieces, shards, tokens, _ = kv_ref.shape
    n_keys = pieces * shards * tokens
    block = n_keys // steps

    @pl.when(pl.program_id(0) == 0)
    def _():
        place = lax.broadcasted_iota(jnp.int32, (n_keys, D), 0)
        piece = place // (shards * tokens)
        shard = place // tokens % shards
        position = (shard * pieces + piece) * tokens + place % tokens
        live = position < live_ref[0]
        k = kv_ref[0].reshape(n_keys, D).astype(jnp.float32)
        v = kv_ref[1].reshape(n_keys, D).astype(jnp.float32)
        k_held[...] = jnp.where(live, k, k[:1]).astype(jnp.bfloat16)
        v_held[:, :D] = jnp.where(live, v, 0.0).astype(jnp.bfloat16)
        v_held[:, D:] = jnp.where(live, 1.0, 0.0).astype(jnp.bfloat16)

    q_all = q_ref[...].reshape(rows, D)
    for start in range(0, rows, sub):
        here = slice(start, start + sub)
        state = (acc_ref[here], peak_ref[here, :1])
        for step in range(steps):
            keys = slice(step * block, (step + 1) * block)
            state = attend_block(q_all[here], k_held[keys], v_held[keys], state)
        out_ref[here] = (state[0][:, :D] / state[0][:, D:]).astype(jnp.bfloat16)


def attend_ref(qkv, acc, peak, kv, live):
    shards, _, tokens, _ = qkv.shape
    n = shards * tokens
    rows, sub = 4 * tokens, tokens
    n_keys = kv.size // (2 * D)
    return pl.pallas_call(
        functools.partial(ref_kernel, rows=rows, sub=sub, steps=2),
        grid=(n // rows,),
        in_specs=[
            whole(pltpu.SMEM),
            pl.BlockSpec((rows // tokens, None, tokens, D), lambda i: (i, 0, 0, 0)),
            pl.BlockSpec((rows, 2 * D), lambda i: (i, 0)),
            pl.BlockSpec((rows, D), lambda i: (i, 0)),
            pl.BlockSpec(kv.shape, lambda i: (0,) * kv.ndim),
        ],
        out_specs=pl.BlockSpec((rows, D), lambda i: (i, 0)),
        out_shape=jax.ShapeDtypeStruct((n, D), jnp.bfloat16),
        scratch_shapes=[
            pltpu.VMEM((n_keys, D), jnp.bfloat16),
            pltpu.VMEM((n_keys, 2 * D), jnp.bfloat16),
        ],
        compiler_params=params(),
        cost_estimate=pl.CostEstimate(
            flops=8 * n * n_keys * D, bytes_accessed=16 * n * D, transcendentals=n * n_keys
        ),
        name="attend_ref",
    )(live, qkv, acc, peak, kv)


def swap(x, axes):
    return lax.all_to_all(x, axes, split_axis=0, concat_axis=0, tiled=True)


def shards(n_grp, n_sp, queries, keys, values, ref_cache, ref_ids, ref_owner, ref_lens):
    live = ref_lens[ref_ids[lax.axis_index("grp")]].reshape(1)

    cache = ref_cache[0]
    width = cache.shape[-1]
    tokens = 2 * cache.shape[1] // n_grp
    held = swap(cache.reshape(n_grp, tokens, width), "grp")

    qkv = swap(pack_heads(queries[0], keys[0], values[0]), "sp")

    routed = route_pieces(ref_ids, ref_owner, held)
    routed = swap(routed.reshape(n_grp * n_sp, tokens, D), ("grp", "sp"))
    kv = routed.reshape(2, n_grp // 2, n_sp, tokens, D)

    acc, peak = attend_own(qkv)
    out = attend_ref(qkv, acc, peak, kv, live)

    back = swap(out.reshape(n_sp, -1, D), "sp")
    return unpack_heads(back)[None]


def solution(mesh):
    in_specs = (
        P("grp", "sp", None),
        P("grp", "sp", None),
        P("grp", "sp", None),
        P("grp", None, "sp", None),
        P(),
        P(),
        P(),
    )
    body = functools.partial(shards, mesh.shape["grp"], mesh.shape["sp"])
    return jax.shard_map(
        body, mesh=mesh, in_specs=in_specs, out_specs=P("grp", "sp", None), check_vma=False
    )
```

time: 372 us -> 151 us (0.41)
  waiting for transfers between devices: 249 us -> 65.9 us
  matrix products: 32.8 us -> 0 us
  Pallas kernels: 0 us -> 30.3 us
  other arithmetic: 19.1 us -> 0 us
  between operations: 17.7 us -> 2.03 us
  local copies, waits for them, and re-layouts: 13.6 us -> 4.88 us
  starting transfers between devices: 21.5 us -> 29.7 us
    all_gather x1 -> x0, waiting for transfers between devices: 216 us -> none  [shards(): lax.all_gather(cache_slot[None], 'grp', axis=0, tiled=True)]
    dot_general x12 -> x0, matrix products: 32.8 us -> none  [the longest x6 22.3 us: one_block(): jnp.einsum('hqk,khd->qhd', soft_probs, value_heads, preferred_element_typ...]
    all_to_all x4 -> x3, waiting for transfers between devices: 33.1 us -> 65.9 us  [swap(): return lax.all_to_all(x, axes, split_axis=0, concat_axis=0, tiled=True)]
    pallas_call x0 -> x5, Pallas kernels: none -> 30.3 us  [the longest x1 13.2 us: attend_own(): pl.pallas_call(functools.partial(own_kernel, rows=rows, sub=sub, steps=4)...]
    reduce_sum x6 -> x0, other arithmetic: 14.3 us -> none  [one_block(): row_total = jnp.sum(weights, axis=-1, keepdims=True)]
    all_to_all x4 -> x3, starting transfers between devices: 21.5 us -> 29.7 us  [swap(): return lax.all_to_all(x, axes, split_axis=0, concat_axis=0, tiled=True)]
    all_to_all x5 -> x0, local copies, waits for them, and re-layouts: 4.73 us -> none  [the longest x1 1.11 us: shards(): lax.all_to_all(values[0], 'sp', split_axis=1, concat_axis=0, tiled=True)]
  transfers between devices with their start and end apart: 5 -> 3, of which waited for: 4 -> 3; matrix products, arithmetic and copies ran while one was open for 4% -> 1% of each run, Pallas kernels for 0% -> 11%
where the time goes in v1:
time: 151 us
  waiting for transfers between devices  65.9 us (44%)
  Pallas kernels  30.3 us (20%)
  starting transfers between devices  29.7 us (20%)
  blocking collectives  17.8 us (12%)
  local copies, waits for them, and re-layouts  4.88 us (3%)
  between operations  2.03 us (1%)
    all_to_all x3, waiting for transfers between devices, swap(): return lax.all_to_all(x, axes, split_axis=0, concat_axis=0, tiled=True)  65.9 us
    all_to_all x3, starting transfers between devices, swap(): return lax.all_to_all(x, axes, split_axis=0, concat_axis=0, tiled=True)  29.7 us
    all_to_all x1, blocking collectives, swap(): return lax.all_to_all(x, axes, split_axis=0, concat_axis=0, tiled=True)  17.8 us
    pallas_call x1, Pallas kernels, attend_own(): pl.pallas_call(functools.partial(own_kernel, rows=rows, sub=sub, steps=4)...  13.2 us
    pallas_call x1, Pallas kernels, attend_ref(): pl.pallas_call(functools.partial(ref_kernel, rows=rows, sub=sub, steps=2)...  12.4 us
    unnamed x16, local copies, waits for them, and re-layouts  3.71 us
  transfers between devices with their start and end apart: 3, of which 3 were waited for; matrix products, arithmetic and copies ran while one was open for 1% of the time, Pallas kernels for 11%

profile of v1, /device:TPU:1, one launch (start us, length us, event | category | flops | bytes accessed | tf_op | source)
XLA Modules:
  0.0 150.6 jit_solution(12702672828573403431)
XLA Ops:
  0.0 0.0 copy-start.1
  0.0 0.0 copy-start
  0.0 11.7 %all-to-all-start.1 = ((bf16[16,16,2048]{2,1,0:T(8,128)(2,1)}), bf16[16,16,2048]{2,1,0:T(8,128)(2,1)S(1)}, u32[]{:S(2)}, u32[]{:S(2)}) async-start(bf16[16,16,2048]{2,1,0:T(8,128)(2,1)} %bitcast.14), calls=%async_computation.1 | async-start | bytes 2097152 | tf_op jit(solution)/shard_map/all_to_all | solution.py:205
  11.7 0.0 copy-done.1
  11.7 0.0 copy-done
  11.7 0.0 copy-start.2
  11.8 1.1 copy-done.2
  12.9 1.9 %pack_heads.1 = bf16[16,3,192,128]{3,2,1,0:T(8,128)(2,1)} custom-call(bf16[192,2048]{1,0:T(8,128)(2,1)S(1)} %bitcast.10, bf16[192,2048]{1,0:T(8,128)(2,1)S(1)} %bitcast.11, bf16[192,2048]{1,0:T(8,128)(2,1)S(1)} %bitcast.12), custom_call_target="tpu_custom_call" | custom-call | bytes 4718592 | tf_op jit(solution)/shard_map/pack_heads/pallas_call | solution.py:36
  14.7 0.0 copy-start.3
  14.7 0.0 copy-start.4
  14.7 23.8 %all-to-all-done.1.held_ref = bf16[16,16,2048]{2,1,0:T(8,128)(2,1)S(1)} async-done(((bf16[16,16,2048]{2,1,0:T(8,128)(2,1)}), bf16[16,16,2048]{2,1,0:T(8,128)(2,1)S(1)}, u32[]{:S(2)}, u32[]{:S(2)}) %all-to-all-start.1) | async-done | bytes 1048608 | tf_op jit(solution)/shard_map/all_to_all | solution.py:205
  38.5 8.8 %all-to-all-start = ((bf16[16,3,192,128]{3,2,1,0:T(8,128)(2,1)}), bf16[16,3,192,128]{3,2,1,0:T(8,128)(2,1)S(1)}, u32[]{:S(2)}, u32[]{:S(2)}) async-start(bf16[16,3,192,128]{3,2,1,0:T(8,128)(2,1)} %pack_heads.1), calls=%async_computation | async-start | bytes 4718592 | tf_op jit(solution)/shard_map/all_to_all | solution.py:205
  47.4 0.0 copy-done.3
  47.4 0.0 copy-done.4
  47.4 0.0 copy-start.7
  47.4 1.8 %route_pieces.1 = bf16[16,16,16,128]{3,2,1,0:T(8,128)(2,1)} custom-call(s32[16]{0:T(128)S(1)} %copy-done.4, s32[16]{0:T(128)S(1)} %copy-done.3, bf16[16,16,2048]{2,1,0:T(8,128)(2,1)S(1)} %all-to-all-done.1.held_ref), custom_call_target="tpu_custom_call" | custom-call | bytes 2097152 | tf_op jit(solution)/shard_map/route_pieces/pallas_call | solution.py:59
  49.2 29.0 %all-to-all-done.q_ref.k_ref.v_ref = bf16[16,3,192,128]{3,2,1,0:T(8,128)(2,1)S(1)} async-done(((bf16[16,3,192,128]{3,2,1,0:T(8,128)(2,1)}), bf16[16,3,192,128]{3,2,1,0:T(8,128)(2,1)S(1)}, u32[]{:S(2)}, u32[]{:S(2)}) %all-to-all-start) | async-done | bytes 2359328 | tf_op jit(solution)/shard_map/all_to_all | solution.py:205
  78.2 9.2 %all-to-all-start.2 = ((bf16[256,16,128]{2,1,0:T(8,128)(2,1)}), bf16[256,16,128]{2,1,0:T(8,128)(2,1)S(1)}, u32[]{:S(2)}, u32[]{:S(2)}) async-start(bf16[256,16,128]{2,1,0:T(8,128)(2,1)} %bitcast.5), calls=%async_computation.2 | async-start | bytes 2097152 | tf_op jit(solution)/shard_map/all_to_all | solution.py:205
  87.4 0.6 dynamic_slice.6
  89.9 0.0 copy-done.7
  89.9 0.6 dynamic_slice.7.live_ref
  90.5 13.2 %attend_own.1 = (f32[3072,256]{1,0:T(8,128)}, f32[3072,128]{1,0:T(8,128)S(1)}) custom-call(bf16[16,3,192,128]{3,2,1,0:T(8,128)(2,1)S(1)} %all-to-all-done.q_ref.k_ref.v_ref, bf16[16,3,192,128]{3,2,1,0:T(8,128)(2,1)S(1)} %all-to-all-done.q_ref.k_ref.v_ref, bf16[16,3,192,128]{3,2,1,0:T(8,128)(2,1)S(1)} %all-to-all-done.q_ref.k_ref.v_ref), custom_call_target="tpu_custom_call" | custom-call | flops 9663676416 | bytes 4718592 | tf_op jit(solution)/shard_map/attend_own/pallas_call | solution.py:121
  103.7 0.0 copy-start.5
  103.7 1.1 copy-done.5
  104.8 13.1 %all-to-all-done.2 = bf16[256,16,128]{2,1,0:T(8,128)(2,1)S(1)} async-done(((bf16[256,16,128]{2,1,0:T(8,128)(2,1)}), bf16[256,16,128]{2,1,0:T(8,128)(2,1)S(1)}, u32[]{:S(2)}, u32[]{:S(2)}) %all-to-all-start.2) | async-done | bytes 1048608 | tf_op jit(solution)/shard_map/all_to_all | solution.py:205
  117.9 0.0 copy-start.6
  117.9 1.4 copy-done.6
  119.3 12.4 %attend_ref.1 = bf16[3072,128]{1,0:T(8,128)(2,1)S(1)} custom-call(s32[1]{0:T(128)} %dynamic_slice.7.live_ref, bf16[16,3,192,128]{3,2,1,0:T(8,128)(2,1)S(1)} %all-to-all-done.q_ref.k_ref.v_ref, f32[3072,256]{1,0:T(8,128)} %get-tuple-element.7.acc_ref, f32[3072,128]{1,0:T(8,128)S(1)} %copy-done.6, bf16[2,8,16,16,128]{4,3,2,1,0:T(8,128)(2,1)S(1)} %bitcast.9), custom_call_target="tpu_custom_call" | custom-call | flops 6442450944 | bytes 6291456 | tf_op jit(solution)/shard_map/attend_ref/pallas_call | solution.py:180
  131.7 17.8 %all_to_all.20.x_ref = bf16[16,192,128]{2,1,0:T(8,128)(2,1)S(1)} all-to-all(bf16[16,192,128]{2,1,0:T(8,128)(2,1)S(1)} %bitcast.13), channel_id=1, replica_groups=mesh['grp'=16,'sp'=16] {'sp'}, dimensions={0} | all-to-all | bytes 1572864 | tf_op jit(solution)/shard_map/all_to_all | solution.py:205
  149.5 1.1 unpack_heads.1
Async XLA Ops:
  0.0 11.7 %copy-start.1 = (bf16[1,192,2048]{2,1,0:T(8,128)(2,1)S(1)}, bf16[1,192,2048]{2,1,0:T(8,128)(2,1)}, u32[]{:S(2)}) copy-start(bf16[1,192,2048]{2,1,0:T(8,128)(2,1)} %param.8) | copy-start | bytes 2359300
  0.0 11.7 %copy-start = (bf16[1,192,2048]{2,1,0:T(8,128)(2,1)S(1)}, bf16[1,192,2048]{2,1,0:T(8,128)(2,1)}, u32[]{:S(2)}) copy-start(bf16[1,192,2048]{2,1,0:T(8,128)(2,1)} %param.7) | copy-start | bytes 2359300
  0.0 38.5 %all-to-all-start.1 = ((bf16[16,16,2048]{2,1,0:T(8,128)(2,1)}), bf16[16,16,2048]{2,1,0:T(8,128)(2,1)S(1)}, u32[]{:S(2)}, u32[]{:S(2)}) async-start(bf16[16,16,2048]{2,1,0:T(8,128)(2,1)} %bitcast.14), calls=%async_computation.1 | async-start | bytes 2097152 | tf_op jit(solution)/shard_map/all_to_all | solution.py:205
  11.7 1.1 copy-start.2
  14.7 32.6 %copy-start.3 = (s32[16]{0:T(128)S(1)}, s32[16]{0:T(128)}, u32[]{:S(2)}) copy-start(s32[16]{0:T(128)} %owner_ref.1) | copy-start | bytes 196
  14.7 32.6 %copy-start.4 = (s32[16]{0:T(128)S(1)}, s32[16]{0:T(128)}, u32[]{:S(2)}) copy-start(s32[16]{0:T(128)} %ids_ref.1) | copy-start | bytes 196
  38.5 39.6 %all-to-all-start = ((bf16[16,3,192,128]{3,2,1,0:T(8,128)(2,1)}), bf16[16,3,192,128]{3,2,1,0:T(8,128)(2,1)S(1)}, u32[]{:S(2)}, u32[]{:S(2)}) async-start(bf16[16,3,192,128]{3,2,1,0:T(8,128)(2,1)} %pack_heads.1), calls=%async_computation | async-start | bytes 4718592 | tf_op jit(solution)/shard_map/all_to_all | solution.py:205
  47.4 42.5 %copy-start.7 = (s32[16]{0:T(128)S(1)}, s32[16]{0:T(128)}, u32[]{:S(2)}) copy-start(s32[16]{0:T(128)} %param.13) | copy-start | bytes 196
  78.2 39.8 %all-to-all-start.2 = ((bf16[256,16,128]{2,1,0:T(8,128)(2,1)}), bf16[256,16,128]{2,1,0:T(8,128)(2,1)S(1)}, u32[]{:S(2)}, u32[]{:S(2)}) async-start(bf16[256,16,128]{2,1,0:T(8,128)(2,1)} %bitcast.5), calls=%async_computation.2 | async-start | bytes 2097152 | tf_op jit(solution)/shard_map/all_to_all | solution.py:205
  103.7 1.2 copy-start.5
  117.9 1.4 copy-start.6

commit v2 on v1

--- a/solution.py
+++ b/solution.py
@@ -44,29 +44,56 @@
     )(q, k, v)
 
 
-def route_kernel(ids_ref, owner_ref, held_ref, out_ref):
-    groups, heads = out_ref.shape[:2]
-    for group in range(groups):
+def spread_kernel(n_z, place_ref, cache_ref, other_ref, *out_refs):
+    z, x = place_ref[0], place_ref[1]
+    tokens = out_refs[0].shape[1]
+    for shift, out_ref in enumerate(out_refs):
+        rows = pl.ds(pl.multiple_of((z + shift) % n_z * tokens, tokens), tokens)
+        out_ref[0] = cache_ref[x, rows]
+        out_ref[1] = other_ref[rows]
+
+
+def spread_pieces(n_z, place, cache, other):
+    _, rows, width = cache.shape
+    piece = jax.ShapeDtypeStruct((2, rows // n_z, width), cache.dtype)
+    return pl.pallas_call(
+        functools.partial(spread_kernel, n_z),
+        in_specs=[whole(pltpu.SMEM), whole(), whole()],
+        out_specs=[whole()] * n_z,
+        out_shape=[piece] * n_z,
+        compiler_params=params(),
+        cost_estimate=pl.CostEstimate(flops=0, bytes_accessed=8 * rows * width, transcendentals=0),
+        name="spread_pieces",
+    )(place, cache, other)
+
+
+def route_kernel(n_z, place_ref, ids_ref, owner_ref, *refs):
+    held_refs, out_ref, held = refs[:n_z], refs[-2], refs[-1]
+    z, x = place_ref[0], place_ref[1]
+    for shift, ref in enumerate(held_refs):
+        held[shift] = ref[...]
+    for group in range(out_ref.shape[0]):
         row = owner_ref[ids_ref[group]]
-        for head in range(heads):
-            out_ref[group, head] = held_ref[row, :, head * D : (head + 1) * D]
-
-
-def route_pieces(ids, owner, held):
-    rows, tokens, width = held.shape
-    groups = ids.shape[0]
-    heads = width // D
-    return pl.pallas_call(
-        route_kernel,
-        in_specs=[whole(pltpu.SMEM), whole(pltpu.SMEM), whole()],
+        shift, side = (z - row // 2 + n_z) % n_z, (row + x) % 2
+        for head in range(out_ref.shape[1]):
+            out_ref[group, head] = held[shift, side, :, head * D : (head + 1) * D]
+
+
+def route_pieces(n_z, place, ids, owner, pieces):
+    piece = pieces[0]
+    _, tokens, width = piece.shape
+    return pl.pallas_call(
+        functools.partial(route_kernel, n_z),
+        in_specs=[whole(pltpu.SMEM)] * 3 + [whole()] * n_z,
         out_specs=whole(),
-        out_shape=jax.ShapeDtypeStruct((groups, heads, tokens, D), held.dtype),
+        out_shape=jax.ShapeDtypeStruct((2 * n_z, width // D, tokens, D), piece.dtype),
+        scratch_shapes=[pltpu.VMEM((n_z, *piece.shape), piece.dtype)],
         compiler_params=params(),
         cost_estimate=pl.CostEstimate(
-            flops=0, bytes_accessed=2 * held.size * 2, transcendentals=0
+            flops=0, bytes_accessed=4 * n_z * piece.size, transcendentals=0
         ),
         name="route_pieces",
-    )(ids, owner, held)
+    )(place, ids, owner, *pieces)
 
 
 def unpack_kernel(x_ref, out_ref):
@@ -145,7 +172,7 @@
 def ref_kernel(
     live_ref, q_ref, acc_ref, peak_ref, kv_ref, out_ref, k_held, v_held, *, rows, sub, steps
 ):
-    halves, pieces, shards, tokens, _ = kv_ref.shape
+    pieces, _, shards, tokens, _ = kv_ref.shape
     n_keys = pieces * shards * tokens
     block = n_keys // steps
 
@@ -156,8 +183,8 @@
         shard = place // tokens % shards
         position = (shard * pieces + piece) * tokens + place % tokens
         live = position < live_ref[0]
-        k = kv_ref[0].reshape(n_keys, D).astype(jnp.float32)
-        v = kv_ref[1].reshape(n_keys, D).astype(jnp.float32)
+        k = kv_ref[:, 0].reshape(n_keys, D).astype(jnp.float32)
+        v = kv_ref[:, 1].reshape(n_keys, D).astype(jnp.float32)
         k_held[...] = jnp.where(live, k, k[:1]).astype(jnp.bfloat16)
         v_held[:, :D] = jnp.where(live, v, 0.0).astype(jnp.bfloat16)
         v_held[:, D:] = jnp.where(live, 1.0, 0.0).astype(jnp.bfloat16)
@@ -205,38 +232,46 @@
     return lax.all_to_all(x, axes, split_axis=0, concat_axis=0, tiled=True)
 
 
-def shards(n_grp, n_sp, queries, keys, values, ref_cache, ref_ids, ref_owner, ref_lens):
-    live = ref_lens[ref_ids[lax.axis_index("grp")]].reshape(1)
+def shift_all(pieces, n_z):
+    moved = list(pieces)
+    for shift in sorted(range(1, n_z), key=lambda s: -min(s, n_z - s)):
+        pairs = [(src, (src + shift) % n_z) for src in range(n_z)]
+        moved[shift] = lax.ppermute(pieces[shift], "z", pairs)
+    return moved
+
+
+def shards(n_z, queries, keys, values, ref_cache, ref_ids, ref_owner, ref_lens):
+    z, x = lax.axis_index("z"), lax.axis_index("x")
+    place = jnp.stack([z, x]).astype(jnp.int32)
+    live = ref_lens[ref_ids[2 * z + x]].reshape(1)
 
     cache = ref_cache[0]
-    width = cache.shape[-1]
-    tokens = 2 * cache.shape[1] // n_grp
-    held = swap(cache.reshape(n_grp, tokens, width), "grp")
-
-    qkv = swap(pack_heads(queries[0], keys[0], values[0]), "sp")
-
-    routed = route_pieces(ref_ids, ref_owner, held)
-    routed = swap(routed.reshape(n_grp * n_sp, tokens, D), ("grp", "sp"))
-    kv = routed.reshape(2, n_grp // 2, n_sp, tokens, D)
+    other = lax.ppermute(lax.dynamic_index_in_dim(cache, 1 - x, 0, keepdims=False), "x", [(0, 1), (1, 0)])
+
+    packed, other = lax.optimization_barrier((pack_heads(queries[0], keys[0], values[0]), other))
+    qkv = swap(packed, "sp")
+
+    held = shift_all(spread_pieces(n_z, place, cache, other), n_z)
+    routed = route_pieces(n_z, place, ref_ids, ref_owner, held)
+    tokens = routed.shape[2]
+    kv = swap(routed.reshape(-1, tokens, D), ("z", "x", "sp")).reshape(n_z, 2, -1, tokens, D)
 
     acc, peak = attend_own(qkv)
     out = attend_ref(qkv, acc, peak, kv, live)
 
-    back = swap(out.reshape(n_sp, -1, D), "sp")
+    back = swap(out.reshape(qkv.shape[0], -1, D), "sp")
     return unpack_heads(back)[None]
 
 
 def solution(mesh):
-    in_specs = (
-        P("grp", "sp", None),
-        P("grp", "sp", None),
-        P("grp", "sp", None),
-        P("grp", None, "sp", None),
-        P(),
-        P(),
-        P(),
+    n_grp, n_sp = mesh.devices.shape
+    n_z = n_grp // 2
+    split = jax.sharding.Mesh(mesh.devices.reshape(n_z, 2, n_sp), ("z", "x", "sp"))
+    token_spec = P(("z", "x"), "sp", None)
+    return jax.shard_map(
+        functools.partial(shards, n_z),
+        mesh=split,
+        in_specs=(token_spec,) * 3 + (P(("z", "x"), None, "sp", None), P(), P(), P()),
+        out_specs=token_spec,
+        check_vma=False,
     )
-    body = functools.partial(shards, mesh.shape["grp"], mesh.shape["sp"])
-    return jax.shard_map(
-        body, mesh=mesh, in_specs=in_specs, out_specs=P("grp", "sp", None), check_vma=False
-    )

time: 151 us -> 137 us (0.907)
  waiting for transfers between devices: 65.9 us -> 35 us
  starting transfers between devices: 29.7 us -> 40.3 us
  local copies, waits for them, and re-layouts: 4.88 us -> 10.1 us
    all_to_all x3 -> x2, waiting for transfers between devices: 65.9 us -> 13.1 us  [swap(): return lax.all_to_all(x, axes, split_axis=0, concat_axis=0, tiled=True)]
    ppermute x0 -> x8, waiting for transfers between devices: none -> 21.9 us  [the longest x7 16.6 us: shift_all(): moved[shift] = lax.ppermute(pieces[shift], 'z', pairs)]
    ppermute x0 -> x8, starting transfers between devices: none -> 21.3 us  [the longest x7 17.6 us: shift_all(): moved[shift] = lax.ppermute(pieces[shift], 'z', pairs)]
    all_to_all x3 -> x2, starting transfers between devices: 29.7 us -> 19.1 us  [swap(): return lax.all_to_all(x, axes, split_axis=0, concat_axis=0, tiled=True)]
    unnamed x16 -> x22, local copies, waits for them, and re-layouts: 3.71 us -> 7.82 us
  transfers between devices with their start and end apart: 3 -> 10, of which waited for: 3 -> 6; matrix products, arithmetic and copies ran while one was open for 1% -> 1% of each run, Pallas kernels for 11% -> 13%
where the time goes in v2:
time: 137 us; the launch traced here: 136 us
  starting transfers between devices  40.3 us (29%)
  waiting for transfers between devices  35 us (26%)
  Pallas kernels  31.1 us (23%)
  blocking collectives  17.8 us (13%)
  local copies, waits for them, and re-layouts  10.1 us (7%)
  between operations  2.02 us (1%)
    all_to_all x2, starting transfers between devices, swap(): return lax.all_to_all(x, axes, split_axis=0, concat_axis=0, tiled=True)  19.1 us
    all_to_all x1, blocking collectives, swap(): return lax.all_to_all(x, axes, split_axis=0, concat_axis=0, tiled=True)  17.8 us
    ppermute x7, starting transfers between devices, shift_all(): moved[shift] = lax.ppermute(pieces[shift], 'z', pairs)  17.6 us
    ppermute x7, waiting for transfers between devices, shift_all(): moved[shift] = lax.ppermute(pieces[shift], 'z', pairs)  16.6 us
    pallas_call x1, Pallas kernels, attend_own(): pl.pallas_call(functools.partial(own_kernel, rows=rows, sub=sub, steps=4)...  13.2 us
    all_to_all x2, waiting for transfers between devices, swap(): return lax.all_to_all(x, axes, split_axis=0, concat_axis=0, tiled=True)  13.1 us
    pallas_call x1, Pallas kernels, attend_ref(): pl.pallas_call(functools.partial(ref_kernel, rows=rows, sub=sub, steps=2)...  12.4 us
    unnamed x22, local copies, waits for them, and re-layouts  7.82 us
  transfers between devices with their start and end apart: 10, of which 6 were waited for; matrix products, arithmetic and copies ran while one was open for 1% of the time, Pallas kernels for 13%

profile of v2, /device:TPU:1, one launch (start us, length us, event | category | flops | bytes accessed | tf_op | source)
XLA Modules:
  0.0 136.4 jit_solution(15598598326703854580)
XLA Ops:
  0.0 1.1 dynamic-slice_bitcast_fusion
  1.1 3.7 %collective-permute-start = (bf16[128,2048]{1,0:T(8,128)(2,1)S(1)}, bf16[128,2048]{1,0:T(8,128)(2,1)S(1)}, u32[]{:S(2)}, u32[]{:S(2)}) collective-permute-start(bf16[128,2048]{1,0:T(8,128)(2,1)S(1)} %dynamic-slice_bitcast_fusion), channel_id=1, source_target_pairs={{0,16},{16,0},{1,17},{17,1},{2,18},{18,2},{3,19},{19,3},{4,20},{20... | collective-permute-start | bytes 1572872 | tf_op jit(solution)/shard_map/ppermute | solution.py:249
  4.8 1.1 copy-done.1
  5.9 1.1 copy-done.2
  7.0 1.1 copy-done.3
  8.2 1.9 %pack_heads.1 = bf16[16,3,192,128]{3,2,1,0:T(8,128)(2,1)} custom-call(bf16[192,2048]{1,0:T(8,128)(2,1)S(1)} %bitcast.15, bf16[192,2048]{1,0:T(8,128)(2,1)S(1)} %bitcast.16, bf16[192,2048]{1,0:T(8,128)(2,1)S(1)} %bitcast.17), custom_call_target="tpu_custom_call" | custom-call | bytes 4718592 | tf_op jit(solution)/shard_map/pack_heads/pallas_call | solution.py:36
  10.0 5.3 %collective-permute-done.other_ref = bf16[128,2048]{1,0:T(8,128)(2,1)S(1)} collective-permute-done((bf16[128,2048]{1,0:T(8,128)(2,1)S(1)}, bf16[128,2048]{1,0:T(8,128)(2,1)S(1)}, u32[]{:S(2)}, u32[]{:S(2)}) %collective-permute-start) | collective-permute-done | bytes 524320 | tf_op jit(solution)/shard_map/ppermute | solution.py:249
  15.3 0.8 copy-done.4
  16.1 7.9 %all-to-all-start = ((bf16[16,3,192,128]{3,2,1,0:T(8,128)(2,1)}), bf16[16,3,192,128]{3,2,1,0:T(8,128)(2,1)S(1)}, u32[]{:S(2)}, u32[]{:S(2)}) async-start(bf16[16,3,192,128]{3,2,1,0:T(8,128)(2,1)} %pack_heads.1), calls=%async_computation | async-start | bytes 4718592 | tf_op jit(solution)/shard_map/all_to_all | solution.py:232
  24.1 1.0 copy-done.5
  25.2 0.6 spread_pieces.1
  25.8 1.7 %collective-permute-start.1 = (bf16[2,16,2048]{2,1,0:T(8,128)(2,1)S(1)}, bf16[2,16,2048]{2,1,0:T(8,128)(2,1)S(1)}, u32[]{:S(2)}, u32[]{:S(2)}) collective-permute-start(bf16[2,16,2048]{2,1,0:T(8,128)(2,1)S(1)} %get-tuple-element.22), channel_id=1, source_target_pairs={{0,32},{32,64},{64,96},{96,128},{128,160},{160,192},{192,224},{224... | collective-permute-start | bytes 393224 | tf_op jit(solution)/shard_map/ppermute | solution.py:239
  27.6 3.0 %collective-permute-start.2 = (bf16[2,16,2048]{2,1,0:T(8,128)(2,1)S(1)}, bf16[2,16,2048]{2,1,0:T(8,128)(2,1)S(1)}, u32[]{:S(2)}, u32[]{:S(2)}) collective-permute-start(bf16[2,16,2048]{2,1,0:T(8,128)(2,1)S(1)} %get-tuple-element.23), channel_id=1, source_target_pairs={{0,64},{32,96},{64,128},{96,160},{128,192},{160,224},{192,0},{224,... | collective-permute-start | bytes 393224 | tf_op jit(solution)/shard_map/ppermute | solution.py:239
  30.5 3.8 %collective-permute-start.3 = (bf16[2,16,2048]{2,1,0:T(8,128)(2,1)S(1)}, bf16[2,16,2048]{2,1,0:T(8,128)(2,1)S(1)}, u32[]{:S(2)}, u32[]{:S(2)}) collective-permute-start(bf16[2,16,2048]{2,1,0:T(8,128)(2,1)S(1)} %get-tuple-element.24), channel_id=1, source_target_pairs={{0,96},{32,128},{64,160},{96,192},{128,224},{160,0},{192,32},{224,... | collective-permute-start | bytes 393224 | tf_op jit(solution)/shard_map/ppermute | solution.py:239
  34.8 4.5 %collective-permute-start.5 = (bf16[2,16,2048]{2,1,0:T(8,128)(2,1)S(1)}, bf16[2,16,2048]{2,1,0:T(8,128)(2,1)S(1)}, u32[]{:S(2)}, u32[]{:S(2)}) collective-permute-start(bf16[2,16,2048]{2,1,0:T(8,128)(2,1)S(1)} %get-tuple-element.26), channel_id=1, source_target_pairs={{0,160},{32,192},{64,224},{96,0},{128,32},{160,64},{192,96},{224,1... | collective-permute-start | bytes 393224 | tf_op jit(solution)/shard_map/ppermute | solution.py:239
  39.2 2.4 %collective-permute-start.6 = (bf16[2,16,2048]{2,1,0:T(8,128)(2,1)S(1)}, bf16[2,16,2048]{2,1,0:T(8,128)(2,1)S(1)}, u32[]{:S(2)}, u32[]{:S(2)}) collective-permute-start(bf16[2,16,2048]{2,1,0:T(8,128)(2,1)S(1)} %get-tuple-element.27), channel_id=1, source_target_pairs={{0,192},{32,224},{64,0},{96,32},{128,64},{160,96},{192,128},{224,1... | collective-permute-start | bytes 393224 | tf_op jit(solution)/shard_map/ppermute | solution.py:239
  41.6 1.8 %collective-permute-start.7 = (bf16[2,16,2048]{2,1,0:T(8,128)(2,1)S(1)}, bf16[2,16,2048]{2,1,0:T(8,128)(2,1)S(1)}, u32[]{:S(2)}, u32[]{:S(2)}) collective-permute-start(bf16[2,16,2048]{2,1,0:T(8,128)(2,1)S(1)} %get-tuple-element.28), channel_id=1, source_target_pairs={{0,224},{32,0},{64,32},{96,64},{128,96},{160,128},{192,160},{224,1... | collective-permute-start | bytes 393224 | tf_op jit(solution)/shard_map/ppermute | solution.py:239
  43.4 7.9 %collective-permute-done.3.refs_3_ = bf16[2,16,2048]{2,1,0:T(8,128)(2,1)S(1)} collective-permute-done((bf16[2,16,2048]{2,1,0:T(8,128)(2,1)S(1)}, bf16[2,16,2048]{2,1,0:T(8,128)(2,1)S(1)}, u32[]{:S(2)}, u32[]{:S(2)}) %collective-permute-start.3) | collective-permute-done | bytes 131104 | tf_op jit(solution)/shard_map/ppermute | solution.py:239
  51.3 0.7 collective-permute-done.4.refs_4_
  52.0 7.5 %collective-permute-done.6.refs_6_ = bf16[2,16,2048]{2,1,0:T(8,128)(2,1)S(1)} collective-permute-done((bf16[2,16,2048]{2,1,0:T(8,128)(2,1)S(1)}, bf16[2,16,2048]{2,1,0:T(8,128)(2,1)S(1)}, u32[]{:S(2)}, u32[]{:S(2)}) %collective-permute-start.6) | collective-permute-done | bytes 131104 | tf_op jit(solution)/shard_map/ppermute | solution.py:239
  59.5 0.5 collective-permute-done.7.refs_7_
  60.0 1.9 %route_pieces.1 = bf16[16,16,16,128]{3,2,1,0:T(8,128)(2,1)} custom-call(s32[2]{0:T(128)S(1)} %pad_add_fusion.place_ref, s32[16]{0:T(128)S(1)} %copy-done.7, s32[16]{0:T(128)S(1)} %copy-done.6, bf16[2,16,2048]{2,1,0:T(8,128)(2,1)S(1)} %get-tuple-element.21.refs_0_, bf16[2,16,2048]{2,1,0:T(8,128)(2,1)S(1)} %collective-permute-done.1.refs_1_, ...), custom_call_target="tpu_custom_call" | custom-call | bytes 2097152 | tf_op jit(solution)/shard_map/route_pieces/pallas_call | solution.py:85
  62.0 11.2 %all-to-all-start.1 = ((bf16[256,16,128]{2,1,0:T(8,128)(2,1)}), bf16[256,16,128]{2,1,0:T(8,128)(2,1)S(1)}, u32[]{:S(2)}, u32[]{:S(2)}) async-start(bf16[256,16,128]{2,1,0:T(8,128)(2,1)} %bitcast.8), calls=%async_computation.1 | async-start | bytes 2097152 | tf_op jit(solution)/shard_map/all_to_all | solution.py:232
  73.1 0.6 dynamic_slice.10
  75.7 0.6 dynamic_slice.11.live_ref
  76.3 13.2 %attend_own.1 = (f32[3072,256]{1,0:T(8,128)}, f32[3072,128]{1,0:T(8,128)S(1)}) custom-call(bf16[16,3,192,128]{3,2,1,0:T(8,128)(2,1)S(1)} %all-to-all-done.q_ref.k_ref.v_ref, bf16[16,3,192,128]{3,2,1,0:T(8,128)(2,1)S(1)} %all-to-all-done.q_ref.k_ref.v_ref, bf16[16,3,192,128]{3,2,1,0:T(8,128)(2,1)S(1)} %all-to-all-done.q_ref.k_ref.v_ref), custom_call_target="tpu_custom_call" | custom-call | flops 9663676416 | bytes 4718592 | tf_op jit(solution)/shard_map/attend_own/pallas_call | solution.py:148
  89.5 1.2 copy-done.8
  90.7 13.1 %all-to-all-done.1 = bf16[256,16,128]{2,1,0:T(8,128)(2,1)S(1)} async-done(((bf16[256,16,128]{2,1,0:T(8,128)(2,1)}), bf16[256,16,128]{2,1,0:T(8,128)(2,1)S(1)}, u32[]{:S(2)}, u32[]{:S(2)}) %all-to-all-start.1) | async-done | bytes 1048608 | tf_op jit(solution)/shard_map/all_to_all | solution.py:232
  103.7 1.4 %copy-done.9 = f32[3072,128]{1,0:T(8,128)S(1)} copy-done((f32[3072,128]{1,0:T(8,128)S(1)}, f32[3072,128]{1,0:T(8,128)}, u32[]{:S(2)}) %copy-start.9) | copy-done | bytes 1572888
  105.1 12.4 %attend_ref.1 = bf16[3072,128]{1,0:T(8,128)(2,1)S(1)} custom-call(s32[1]{0:T(128)} %dynamic_slice.11.live_ref, bf16[16,3,192,128]{3,2,1,0:T(8,128)(2,1)S(1)} %all-to-all-done.q_ref.k_ref.v_ref, f32[3072,256]{1,0:T(8,128)} %get-tuple-element.18.acc_ref, f32[3072,128]{1,0:T(8,128)S(1)} %copy-done.9, bf16[8,2,16,16,128]{4,3,2,1,0:T(8,128)(2,1)S(1)} %bitcast.14), custom_call_target="tpu_custom_call" | custom-call | flops 6442450944 | bytes 6291456 | tf_op jit(solution)/shard_map/attend_ref/pallas_call | solution.py:207
  117.5 17.8 %all_to_all.15.x_ref = bf16[16,192,128]{2,1,0:T(8,128)(2,1)S(1)} all-to-all(bf16[16,192,128]{2,1,0:T(8,128)(2,1)S(1)} %bitcast.18), channel_id=1, replica_groups=mesh['z'=8,'x'=2,'sp'=16] {'sp'}, dimensions={0} | all-to-all | bytes 1572864 | tf_op jit(solution)/shard_map/all_to_all | solution.py:232
  135.3 1.1 unpack_heads.1
  (21 shorter events, 0.6 us)
Async XLA Ops:
  1.1 14.3 %collective-permute-start = (bf16[128,2048]{1,0:T(8,128)(2,1)S(1)}, bf16[128,2048]{1,0:T(8,128)(2,1)S(1)}, u32[]{:S(2)}, u32[]{:S(2)}) collective-permute-start(bf16[128,2048]{1,0:T(8,128)(2,1)S(1)} %dynamic-slice_bitcast_fusion), channel_id=1, source_target_pairs={{0,16},{16,0},{1,17},{17,1},{2,18},{18,2},{3,19},{19,3},{4,20},{20... | collective-permute-start | bytes 1572872 | tf_op jit(solution)/shard_map/ppermute | solution.py:249
  4.7 1.1 copy-start.1
  5.9 1.1 copy-start.2
  7.0 1.1 copy-start.3
  10.0 14.1 %copy-start = (bf16[1,2,128,2048]{3,2,1,0:T(8,128)(2,1)S(1)}, bf16[1,2,128,2048]{3,2,1,0:T(8,128)(2,1)}, u32[]{:S(2)}) copy-start(bf16[1,2,128,2048]{3,2,1,0:T(8,128)(2,1)} %param.10) | copy-start | bytes 3145732
  10.0 50.0 %copy-start.6 = (s32[16]{0:T(128)S(1)}, s32[16]{0:T(128)}, u32[]{:S(2)}) copy-start(s32[16]{0:T(128)} %owner_ref.1) | copy-start | bytes 196
  10.0 50.0 %copy-start.7 = (s32[16]{0:T(128)S(1)}, s32[16]{0:T(128)}, u32[]{:S(2)}) copy-start(s32[16]{0:T(128)} %ids_ref.1) | copy-start | bytes 196
  15.3 0.8 copy-start.4
  16.1 45.8 %all-to-all-start = ((bf16[16,3,192,128]{3,2,1,0:T(8,128)(2,1)}), bf16[16,3,192,128]{3,2,1,0:T(8,128)(2,1)S(1)}, u32[]{:S(2)}, u32[]{:S(2)}) async-start(bf16[16,3,192,128]{3,2,1,0:T(8,128)(2,1)} %pack_heads.1), calls=%async_computation | async-start | bytes 4718592 | tf_op jit(solution)/shard_map/all_to_all | solution.py:232
  24.1 1.0 copy-start.5
  25.8 49.9 %copy-start.10 = (s32[16]{0:T(128)S(1)}, s32[16]{0:T(128)}, u32[]{:S(2)}) copy-start(s32[16]{0:T(128)} %param.13) | copy-start | bytes 196
  25.8 13.4 %collective-permute-start.1 = (bf16[2,16,2048]{2,1,0:T(8,128)(2,1)S(1)}, bf16[2,16,2048]{2,1,0:T(8,128)(2,1)S(1)}, u32[]{:S(2)}, u32[]{:S(2)}) collective-permute-start(bf16[2,16,2048]{2,1,0:T(8,128)(2,1)S(1)} %get-tuple-element.22), channel_id=1, source_target_pairs={{0,32},{32,64},{64,96},{96,128},{128,160},{160,192},{192,224},{224... | collective-permute-start | bytes 393224 | tf_op jit(solution)/shard_map/ppermute | solution.py:239
  27.6 14.1 %collective-permute-start.2 = (bf16[2,16,2048]{2,1,0:T(8,128)(2,1)S(1)}, bf16[2,16,2048]{2,1,0:T(8,128)(2,1)S(1)}, u32[]{:S(2)}, u32[]{:S(2)}) collective-permute-start(bf16[2,16,2048]{2,1,0:T(8,128)(2,1)S(1)} %get-tuple-element.23), channel_id=1, source_target_pairs={{0,64},{32,96},{64,128},{96,160},{128,192},{160,224},{192,0},{224,... | collective-permute-start | bytes 393224 | tf_op jit(solution)/shard_map/ppermute | solution.py:239
  30.5 20.7 %collective-permute-start.3 = (bf16[2,16,2048]{2,1,0:T(8,128)(2,1)S(1)}, bf16[2,16,2048]{2,1,0:T(8,128)(2,1)S(1)}, u32[]{:S(2)}, u32[]{:S(2)}) collective-permute-start(bf16[2,16,2048]{2,1,0:T(8,128)(2,1)S(1)} %get-tuple-element.24), channel_id=1, source_target_pairs={{0,96},{32,128},{64,160},{96,192},{128,224},{160,0},{192,32},{224,... | collective-permute-start | bytes 393224 | tf_op jit(solution)/shard_map/ppermute | solution.py:239
  34.3 17.7 %collective-permute-start.4 = (bf16[2,16,2048]{2,1,0:T(8,128)(2,1)S(1)}, bf16[2,16,2048]{2,1,0:T(8,128)(2,1)S(1)}, u32[]{:S(2)}, u32[]{:S(2)}) collective-permute-start(bf16[2,16,2048]{2,1,0:T(8,128)(2,1)S(1)} %get-tuple-element.25), channel_id=1, source_target_pairs={{0,128},{32,160},{64,192},{96,224},{128,0},{160,32},{192,64},{224,... | collective-permute-start | bytes 393224 | tf_op jit(solution)/shard_map/ppermute | solution.py:239
  34.8 17.3 %collective-permute-start.5 = (bf16[2,16,2048]{2,1,0:T(8,128)(2,1)S(1)}, bf16[2,16,2048]{2,1,0:T(8,128)(2,1)S(1)}, u32[]{:S(2)}, u32[]{:S(2)}) collective-permute-start(bf16[2,16,2048]{2,1,0:T(8,128)(2,1)S(1)} %get-tuple-element.26), channel_id=1, source_target_pairs={{0,160},{32,192},{64,224},{96,0},{128,32},{160,64},{192,96},{224,1... | collective-permute-start | bytes 393224 | tf_op jit(solution)/shard_map/ppermute | solution.py:239
  39.2 20.3 %collective-permute-start.6 = (bf16[2,16,2048]{2,1,0:T(8,128)(2,1)S(1)}, bf16[2,16,2048]{2,1,0:T(8,128)(2,1)S(1)}, u32[]{:S(2)}, u32[]{:S(2)}) collective-permute-start(bf16[2,16,2048]{2,1,0:T(8,128)(2,1)S(1)} %get-tuple-element.27), channel_id=1, source_target_pairs={{0,192},{32,224},{64,0},{96,32},{128,64},{160,96},{192,128},{224,1... | collective-permute-start | bytes 393224 | tf_op jit(solution)/shard_map/ppermute | solution.py:239
  41.6 18.4 %collective-permute-start.7 = (bf16[2,16,2048]{2,1,0:T(8,128)(2,1)S(1)}, bf16[2,16,2048]{2,1,0:T(8,128)(2,1)S(1)}, u32[]{:S(2)}, u32[]{:S(2)}) collective-permute-start(bf16[2,16,2048]{2,1,0:T(8,128)(2,1)S(1)} %get-tuple-element.28), channel_id=1, source_target_pairs={{0,224},{32,0},{64,32},{96,64},{128,96},{160,128},{192,160},{224,1... | collective-permute-start | bytes 393224 | tf_op jit(solution)/shard_map/ppermute | solution.py:239
  62.0 41.7 %all-to-all-start.1 = ((bf16[256,16,128]{2,1,0:T(8,128)(2,1)}), bf16[256,16,128]{2,1,0:T(8,128)(2,1)S(1)}, u32[]{:S(2)}, u32[]{:S(2)}) async-start(bf16[256,16,128]{2,1,0:T(8,128)(2,1)} %bitcast.8), calls=%async_computation.1 | async-start | bytes 2097152 | tf_op jit(solution)/shard_map/all_to_all | solution.py:232
  89.5 1.2 copy-start.8
  103.7 1.4 %copy-start.9 = (f32[3072,128]{1,0:T(8,128)S(1)}, f32[3072,128]{1,0:T(8,128)}, u32[]{:S(2)}) copy-start(f32[3072,128]{1,0:T(8,128)} %copy-done.8) | copy-start | bytes 4718596

commit v3 on v2

v3 whole, which is shorter than its diff:
```python
import functools
import math

import jax
import jax.numpy as jnp
from jax import lax
from jax.experimental import pallas as pl
from jax.experimental.pallas import tpu as pltpu
from jax.sharding import PartitionSpec as P

D = 128
EXP_SCALE = D**-0.5 * math.log2(math.e)
ROWS_CONTRACT = (((1,), (1,)), ((), ()))
VMEM_LIMIT = 24 << 20
PER_ROW = 8


def params():
    return pltpu.CompilerParams(vmem_limit_bytes=VMEM_LIMIT)


def whole(memory_space=pltpu.VMEM):
    return pl.BlockSpec(memory_space=memory_space)


def pack_kernel(q_ref, k_ref, v_ref, out_ref):
    for head in range(out_ref.shape[0]):
        cols = slice(head * D, (head + 1) * D)
        for which, ref in enumerate((q_ref, k_ref, v_ref)):
            out_ref[head, which] = ref[:, cols]


def pack_heads(q, k, v):
    tokens, width = q.shape
    heads = width // D
    return pl.pallas_call(
        pack_kernel,
        in_specs=[whole()] * 3,
        out_specs=whole(),
        out_shape=jax.ShapeDtypeStruct((heads, 3, tokens, D), q.dtype),
        compiler_params=params(),
        cost_estimate=pl.CostEstimate(flops=0, bytes_accessed=12 * q.size, transcendentals=0),
        name="pack_heads",
    )(q, k, v)


def spread_kernel(n_z, shifts, place_ref, cache_ref, other_ref, *out_refs):
    z, x = place_ref[0], place_ref[1]
    for shift, out_ref in zip(shifts, out_refs):
        tokens = out_ref.shape[1]
        here = pl.ds(pl.multiple_of((z + shift) % n_z * tokens, tokens), tokens)
        out_ref[0] = cache_ref[x, here]
        out_ref[1] = other_ref[here]


def spread_pieces(n_z, place, shifts, cache, other):
    piece = jax.ShapeDtypeStruct((2, cache.shape[1] // n_z, cache.shape[2]), cache.dtype)
    return pl.pallas_call(
        functools.partial(spread_kernel, n_z, shifts),
        in_specs=[whole(pltpu.SMEM), whole(), whole()],
        out_specs=[whole()] * n_z,
        out_shape=[piece] * n_z,
        compiler_params=params(),
        cost_estimate=pl.CostEstimate(flops=0, bytes_accessed=4 * cache.size, transcendentals=0),
        name="spread_pieces",
    )(place, cache, other)


def route_kernel(n_z, shifts, place_ref, ids_ref, owner_ref, *refs):
    out_ref, held = refs[-2:]
    z, x = place_ref[0], place_ref[1]
    for shift, ref in zip(shifts, refs[:-2]):
        held[shift] = ref[0]
        held[n_z + shift] = ref[1]
    for group in range(out_ref.shape[0]):
        row = owner_ref[ids_ref[group]]
        slot = (row + x) % 2 * n_z + (z - row // 2 + n_z) % n_z
        for head in range(out_ref.shape[1]):
            out_ref[group, head] = held[slot, :, head * D : (head + 1) * D]


def route_pieces(n_z, place, ids, owner, pieces, shifts):
    _, tokens, width = pieces[0].shape
    return pl.pallas_call(
        functools.partial(route_kernel, n_z, shifts),
        in_specs=[whole(pltpu.SMEM)] * 3 + [whole()] * len(pieces),
        out_specs=whole(),
        out_shape=jax.ShapeDtypeStruct((2 * n_z, width // D, tokens, D), pieces[0].dtype),
        scratch_shapes=[pltpu.VMEM((2 * n_z, tokens, width), pieces[0].dtype)],
        compiler_params=params(),
        cost_estimate=pl.CostEstimate(
            flops=0, bytes_accessed=8 * n_z * tokens * width, transcendentals=0
        ),
        name="route_pieces",
    )(place, ids, owner, *pieces)


def unpack_kernel(x_ref, out_ref):
    for head in range(x_ref.shape[0]):
        out_ref[:, head * D : (head + 1) * D] = x_ref[head]


def unpack_heads(x):
    heads, tokens, _ = x.shape
    return pl.pallas_call(
        unpack_kernel,
        in_specs=[whole()],
        out_specs=whole(),
        out_shape=jax.ShapeDtypeStruct((tokens, heads * D), x.dtype),
        compiler_params=params(),
        name="unpack_heads",
    )(x)


def attend_block(q, k, v_ones, state):
    s = lax.dot_general(q, k, ROWS_CONTRACT, preferred_element_type=jnp.float32)
    peak = jnp.max(s, axis=1, keepdims=True)
    if state is not None:
        peak = jnp.maximum(state[1], peak)
    p = jnp.exp2((s - peak) * EXP_SCALE).astype(jnp.bfloat16)
    part = jnp.dot(p, v_ones, preferred_element_type=jnp.float32)
    if state is not None:
        part = state[0] * jnp.exp2((state[1] - peak) * EXP_SCALE) + part
    return part, peak


def own_kernel(qkv_ref, acc_ref, stats_ref, *, per_row, steps):
    shards, _, tokens, _ = qkv_ref.shape
    per = shards // steps
    base = pl.program_id(0) * per_row
    for i in range(per_row):
        q = qkv_ref[base + i, 0]
        state = None
        for step in range(steps):
            here = slice(step * per, (step + 1) * per)
            k = qkv_ref[here, 1].reshape(per * tokens, D)
            v = qkv_ref[here, 2].reshape(per * tokens, D)
            v_ones = jnp.concatenate([v, jnp.ones_like(v)], axis=1)
            state = attend_block(q, k, v_ones, state)
        acc_ref[base + i] = state[0][:, :D]
        column = lax.broadcasted_iota(jnp.int32, (tokens, D), 1)
        stats = jnp.where(column == 0, state[0][:, D:], state[1])
        stats_ref[base + i] = jnp.transpose(stats)[: stats_ref.shape[1]]


def attend_own(qkv):
    shards, _, tokens, _ = qkv.shape
    n = shards * tokens
    return pl.pallas_call(
        functools.partial(own_kernel, per_row=PER_ROW, steps=4),
        grid=(shards // PER_ROW,),
        in_specs=[whole()],
        out_specs=[whole()] * 2,
        out_shape=[
            jax.ShapeDtypeStruct((shards, tokens, D), jnp.float32),
            jax.ShapeDtypeStruct((shards, 8, tokens), jnp.float32),
        ],
        compiler_params=params(),
        cost_estimate=pl.CostEstimate(
            flops=8 * n * n * D, bytes_accessed=12 * n * D, transcendentals=n * n
        ),
        name="attend_own",
    )(qkv)


def ref_kernel(
    live_ref, qkv_ref, acc_ref, stats_ref, kv_ref, out_ref, k_held, v_held, *, per_row, steps
):
    pieces, _, shards, tokens, _ = kv_ref.shape
    n_keys = pieces * shards * tokens
    block = n_keys // steps

    @pl.when(pl.program_id(0) == 0)
    def _():
        for piece in range(pieces):
            for shard in range(shards):
                start = (shard * pieces + piece) * tokens
                k_held[start : start + tokens] = kv_ref[piece, 0, shard]
                v_held[start : start + tokens, :D] = kv_ref[piece, 1, shard]
        v_held[:, D:] = jnp.ones((n_keys, D), jnp.bfloat16)

        for start in range(0, n_keys, block):
            keys = slice(start, start + block)

            @pl.when(live_ref[0] < start + block)
            def _():
                live = lax.broadcasted_iota(jnp.int32, (block, D), 0) + start < live_ref[0]
                k = k_held[keys].astype(jnp.float32)
                first = k_held[:tokens].astype(jnp.float32)[:1]
                k_held[keys] = jnp.where(live, k, first).astype(jnp.bfloat16)
                v = v_held[keys, :D].astype(jnp.float32)
                v_held[keys, :D] = jnp.where(live, v, 0.0).astype(jnp.bfloat16)
                v_held[keys, D:] = jnp.where(live, 1.0, 0.0).astype(jnp.bfloat16)

    base = pl.program_id(0) * per_row
    rows = qkv_ref.shape[2]
    for i in range(per_row):
        q = qkv_ref[base + i, 0]
        stats = stats_ref[base + i]
        total, peak = (
            jnp.transpose(jnp.broadcast_to(stats[j : j + 1], (D, rows))) for j in range(2)
        )
        state = (jnp.concatenate([acc_ref[base + i], total], axis=1), peak[:, :1])
        for step in range(steps):
            keys = slice(step * block, (step + 1) * block)
            state = attend_block(q, k_held[keys], v_held[keys], state)
        out_ref[base + i] = (state[0][:, :D] / state[0][:, D:]).astype(jnp.bfloat16)


def attend_ref(qkv, acc, stats, kv, live):
    shards, _, tokens, _ = qkv.shape
    n = shards * tokens
    n_keys = kv.size // (2 * D)
    return pl.pallas_call(
        functools.partial(ref_kernel, per_row=PER_ROW, steps=2),
        grid=(shards // PER_ROW,),
        in_specs=[whole(pltpu.SMEM)] + [whole()] * 4,
        out_specs=whole(),
        out_shape=jax.ShapeDtypeStruct((shards, tokens, D), jnp.bfloat16),
        scratch_shapes=[
            pltpu.VMEM((n_keys, D), jnp.bfloat16),
            pltpu.VMEM((n_keys, 2 * D), jnp.bfloat16),
        ],
        compiler_params=params(),
        cost_estimate=pl.CostEstimate(
            flops=8 * n * n_keys * D, bytes_accessed=16 * n * D, transcendentals=n * n_keys
        ),
        name="attend_ref",
    )(live, qkv, acc, stats, kv)


def swap(x, axes):
    return lax.all_to_all(x, axes, split_axis=0, concat_axis=0, tiled=True)


def shift_z(piece, shift, n_z):
    if shift == 0:
        return piece
    return lax.ppermute(piece, "z", [(src, (src + shift) % n_z) for src in range(n_z)])


def shards(n_z, queries, keys, values, ref_cache, ref_ids, ref_owner, ref_lens):
    z, x = lax.axis_index("z"), lax.axis_index("x")
    place = jnp.stack([z, x]).astype(jnp.int32)
    live = ref_lens[ref_ids[2 * z + x]].reshape(1)

    cache = ref_cache[0]
    other = lax.dynamic_index_in_dim(cache, 1 - x, 0, keepdims=False)
    other = lax.ppermute(other, "x", [(0, 1), (1, 0)])

    shifts = sorted(range(n_z), key=lambda shift: -min(shift, n_z - shift))
    sent = spread_pieces(n_z, place, shifts, cache, other)

    packed = pack_heads(queries[0], keys[0], values[0])
    packed, sent = lax.optimization_barrier((packed, sent))
    qkv = swap(packed, "sp")
    held = [shift_z(piece, shift, n_z) for piece, shift in zip(sent, shifts)]

    routed = route_pieces(n_z, place, ref_ids, ref_owner, held, shifts)
    tokens = routed.shape[2]
    kv = swap(routed.reshape(-1, tokens, D), ("z", "x", "sp")).reshape(n_z, 2, -1, tokens, D)

    out = attend_ref(qkv, *attend_own(qkv), kv, live)

    back = swap(out, "sp")
    return unpack_heads(back)[None]


def solution(mesh):
    n_grp, n_sp = mesh.devices.shape
    n_z = n_grp // 2
    split = jax.sharding.Mesh(mesh.devices.reshape(n_z, 2, n_sp), ("z", "x", "sp"))
    token_spec = P(("z", "x"), "sp", None)
    return jax.shard_map(
        functools.partial(shards, n_z),
        mesh=split,
        in_specs=(token_spec,) * 3 + (P(("z", "x"), None, "sp", None), P(), P(), P()),
        out_specs=token_spec,
        check_vma=False,
    )
```

time: 137 us -> 134 us (0.978)
  Pallas kernels: 31.1 us -> 27.7 us
  local copies, waits for them, and re-layouts: 10.1 us -> 8.24 us
  starting transfers between devices: 40.3 us -> 41.8 us
    pallas_call x4, Pallas kernels: 28.1 us -> 24.7 us  [the longest x1 11.4 us: attend_own(): pl.pallas_call(functools.partial(own_kernel, per_row=PER_ROW, steps=4), g...]
    all_to_all x2, starting transfers between devices: 19.1 us -> 22.3 us  [swap(): return lax.all_to_all(x, axes, split_axis=0, concat_axis=0, tiled=True)]
    all_to_all x2, waiting for transfers between devices: 13.1 us -> 14.9 us  [swap(): return lax.all_to_all(x, axes, split_axis=0, concat_axis=0, tiled=True)]
    unnamed x22 -> x18, local copies, waits for them, and re-layouts: 7.82 us -> 6 us
    ppermute x8, starting transfers between devices: 21.3 us -> 19.5 us  [the longest x7 15.8 us: shift_z(): lax.ppermute(piece, 'z', [(src, (src + shift) % n_z) for src in range(n_z)])]
    ppermute x8, waiting for transfers between devices: 21.9 us -> 20.5 us  [the longest x7 15.2 us: shift_z(): lax.ppermute(piece, 'z', [(src, (src + shift) % n_z) for src in range(n_z)])]
  transfers between devices with their start and end apart: 10 -> 10, of which waited for: 6 -> 7; matrix products, arithmetic and copies ran while one was open for 1% -> 1% of each run, Pallas kernels for 13% -> 11%
where the time goes in v3:
time: 134 us; the launch traced here: 133 us
  starting transfers between devices  41.8 us (31%)
  waiting for transfers between devices  35.3 us (26%)
  Pallas kernels  27.7 us (21%)
  blocking collectives  17.8 us (13%)
  local copies, waits for them, and re-layouts  8.24 us (6%)
  between operations  2.03 us (2%)
    all_to_all x2, starting transfers between devices, swap(): return lax.all_to_all(x, axes, split_axis=0, concat_axis=0, tiled=True)  22.3 us
    all_to_all x1, blocking collectives, swap(): return lax.all_to_all(x, axes, split_axis=0, concat_axis=0, tiled=True)  17.8 us
    ppermute x7, starting transfers between devices, shift_z(): lax.ppermute(piece, 'z', [(src, (src + shift) % n_z) for src in range(n_z)])  15.8 us
    ppermute x7, waiting for transfers between devices, shift_z(): lax.ppermute(piece, 'z', [(src, (src + shift) % n_z) for src in range(n_z)])  15.2 us
    all_to_all x2, waiting for transfers between devices, swap(): return lax.all_to_all(x, axes, split_axis=0, concat_axis=0, tiled=True)  14.9 us
    pallas_call x1, Pallas kernels, attend_own(): pl.pallas_call(functools.partial(own_kernel, per_row=PER_ROW, steps=4), g...  11.4 us
    pallas_call x1, Pallas kernels, attend_ref(): pl.pallas_call(functools.partial(ref_kernel, per_row=PER_ROW, steps=2), g...  10.8 us
    unnamed x18, local copies, waits for them, and re-layouts  6 us
  transfers between devices with their start and end apart: 10, of which 7 were waited for; matrix products, arithmetic and copies ran while one was open for 1% of the time, Pallas kernels for 11%

profile of v3, /device:TPU:1, one launch (start us, length us, event | category | flops | bytes accessed | tf_op | source)
XLA Modules:
  0.0 132.9 jit_solution(9545705103871373696)
XLA Ops:
  0.0 1.1 dynamic-slice_bitcast_fusion
  1.1 3.7 %collective-permute-start = (bf16[128,2048]{1,0:T(8,128)(2,1)S(1)}, bf16[128,2048]{1,0:T(8,128)(2,1)S(1)}, u32[]{:S(2)}, u32[]{:S(2)}) collective-permute-start(bf16[128,2048]{1,0:T(8,128)(2,1)S(1)} %dynamic-slice_bitcast_fusion), channel_id=1, source_target_pairs={{0,16},{16,0},{1,17},{17,1},{2,18},{18,2},{3,19},{19,3},{4,20},{20... | collective-permute-start | bytes 1572872 | tf_op jit(solution)/shard_map/ppermute | solution.py:249
  4.7 1.1 copy-done.1
  5.9 1.1 copy-done.2
  7.0 1.1 copy-done.3
  8.1 1.9 %pack_heads.1 = bf16[16,3,192,128]{3,2,1,0:T(8,128)(2,1)} custom-call(bf16[192,2048]{1,0:T(8,128)(2,1)S(1)} %bitcast.14, bf16[192,2048]{1,0:T(8,128)(2,1)S(1)} %bitcast.15, bf16[192,2048]{1,0:T(8,128)(2,1)S(1)} %bitcast.16), custom_call_target="tpu_custom_call" | custom-call | bytes 4718592 | tf_op jit(solution)/shard_map/pack_heads/pallas_call | solution.py:36
  10.0 0.1 pad_add_fusion.place_ref
  10.1 5.2 %collective-permute-done.other_ref = bf16[128,2048]{1,0:T(8,128)(2,1)S(1)} collective-permute-done((bf16[128,2048]{1,0:T(8,128)(2,1)S(1)}, bf16[128,2048]{1,0:T(8,128)(2,1)S(1)}, u32[]{:S(2)}, u32[]{:S(2)}) %collective-permute-start) | collective-permute-done | bytes 524320 | tf_op jit(solution)/shard_map/ppermute | solution.py:249
  15.3 0.6 spread_pieces.1
  16.0 7.9 %all-to-all-start = ((bf16[16,3,192,128]{3,2,1,0:T(8,128)(2,1)}), bf16[16,3,192,128]{3,2,1,0:T(8,128)(2,1)S(1)}, u32[]{:S(2)}, u32[]{:S(2)}) async-start(bf16[16,3,192,128]{3,2,1,0:T(8,128)(2,1)} %pack_heads.1), calls=%async_computation | async-start | bytes 4718592 | tf_op jit(solution)/shard_map/all_to_all | solution.py:233
  23.9 7.0 %collective-permute-start.1 = (bf16[2,16,2048]{2,1,0:T(8,128)(2,1)S(1)}, bf16[2,16,2048]{2,1,0:T(8,128)(2,1)S(1)}, u32[]{:S(2)}, u32[]{:S(2)}) collective-permute-start(bf16[2,16,2048]{2,1,0:T(8,128)(2,1)S(1)} %get-tuple-element.35), channel_id=1, source_target_pairs={{0,128},{32,160},{64,192},{96,224},{128,0},{160,32},{192,64},{224,... | collective-permute-start | bytes 393224 | tf_op jit(solution)/shard_map/ppermute | solution.py:239
  30.9 1.6 %collective-permute-start.2 = (bf16[2,16,2048]{2,1,0:T(8,128)(2,1)S(1)}, bf16[2,16,2048]{2,1,0:T(8,128)(2,1)S(1)}, u32[]{:S(2)}, u32[]{:S(2)}) collective-permute-start(bf16[2,16,2048]{2,1,0:T(8,128)(2,1)S(1)} %get-tuple-element.36), channel_id=1, source_target_pairs={{0,96},{32,128},{64,160},{96,192},{128,224},{160,0},{192,32},{224,... | collective-permute-start | bytes 393224 | tf_op jit(solution)/shard_map/ppermute | solution.py:239
  32.6 2.8 %collective-permute-start.3 = (bf16[2,16,2048]{2,1,0:T(8,128)(2,1)S(1)}, bf16[2,16,2048]{2,1,0:T(8,128)(2,1)S(1)}, u32[]{:S(2)}, u32[]{:S(2)}) collective-permute-start(bf16[2,16,2048]{2,1,0:T(8,128)(2,1)S(1)} %get-tuple-element.37), channel_id=1, source_target_pairs={{0,160},{32,192},{64,224},{96,0},{128,32},{160,64},{192,96},{224,1... | collective-permute-start | bytes 393224 | tf_op jit(solution)/shard_map/ppermute | solution.py:239
  35.4 1.2 collective-permute-start.4
  36.6 2.4 %collective-permute-start.5 = (bf16[2,16,2048]{2,1,0:T(8,128)(2,1)S(1)}, bf16[2,16,2048]{2,1,0:T(8,128)(2,1)S(1)}, u32[]{:S(2)}, u32[]{:S(2)}) collective-permute-start(bf16[2,16,2048]{2,1,0:T(8,128)(2,1)S(1)} %get-tuple-element.39), channel_id=1, source_target_pairs={{0,192},{32,224},{64,0},{96,32},{128,64},{160,96},{192,128},{224,1... | collective-permute-start | bytes 393224 | tf_op jit(solution)/shard_map/ppermute | solution.py:239
  39.0 0.7 collective-permute-start.6
  39.7 7.2 %collective-permute-done.2.refs_1_ = bf16[2,16,2048]{2,1,0:T(8,128)(2,1)S(1)} collective-permute-done((bf16[2,16,2048]{2,1,0:T(8,128)(2,1)S(1)}, bf16[2,16,2048]{2,1,0:T(8,128)(2,1)S(1)}, u32[]{:S(2)}, u32[]{:S(2)}) %collective-permute-start.2) | collective-permute-done | bytes 131104 | tf_op jit(solution)/shard_map/ppermute | solution.py:239
  47.0 1.3 collective-permute-done.4.refs_3_
  48.2 3.3 %collective-permute-done.5.refs_4_ = bf16[2,16,2048]{2,1,0:T(8,128)(2,1)S(1)} collective-permute-done((bf16[2,16,2048]{2,1,0:T(8,128)(2,1)S(1)}, bf16[2,16,2048]{2,1,0:T(8,128)(2,1)S(1)}, u32[]{:S(2)}, u32[]{:S(2)}) %collective-permute-start.5) | collective-permute-done | bytes 131104 | tf_op jit(solution)/shard_map/ppermute | solution.py:239
  51.6 2.7 %collective-permute-done.6.refs_5_ = bf16[2,16,2048]{2,1,0:T(8,128)(2,1)S(1)} collective-permute-done((bf16[2,16,2048]{2,1,0:T(8,128)(2,1)S(1)}, bf16[2,16,2048]{2,1,0:T(8,128)(2,1)S(1)}, u32[]{:S(2)}, u32[]{:S(2)}) %collective-permute-start.6) | collective-permute-done | bytes 131104 | tf_op jit(solution)/shard_map/ppermute | solution.py:239
  54.3 0.7 collective-permute-done.7.refs_6_
  55.0 1.9 %route_pieces.1 = bf16[16,16,16,128]{3,2,1,0:T(8,128)(2,1)} custom-call(s32[2]{0:T(128)S(1)} %pad_add_fusion.place_ref, s32[16]{0:T(128)S(1)} %copy-done.5, s32[16]{0:T(128)S(1)} %copy-done.4, bf16[2,16,2048]{2,1,0:T(8,128)(2,1)S(1)} %collective-permute-done.1.refs_0_, bf16[2,16,2048]{2,1,0:T(8,128)(2,1)S(1)} %collective-permute-done.2.refs_1_, ...), custom_call_target="tpu_custom_call" | custom-call | bytes 2097152 | tf_op jit(solution)/shard_map/route_pieces/pallas_call | solution.py:84
  56.9 14.4 %all-to-all-start.1 = ((bf16[256,16,128]{2,1,0:T(8,128)(2,1)}), bf16[256,16,128]{2,1,0:T(8,128)(2,1)S(1)}, u32[]{:S(2)}, u32[]{:S(2)}) async-start(bf16[256,16,128]{2,1,0:T(8,128)(2,1)} %bitcast.8), calls=%async_computation.1 | async-start | bytes 2097152 | tf_op jit(solution)/shard_map/all_to_all | solution.py:233
  71.2 0.6 dynamic_slice.10
  73.8 0.6 dynamic_slice.11.live_ref
  74.4 11.4 %attend_own.1 = (f32[16,192,128]{2,1,0:T(8,128)S(1)}, f32[16,8,192]{2,1,0:T(8,128)S(1)}) custom-call(bf16[16,3,192,128]{3,2,1,0:T(8,128)(2,1)S(1)} %all-to-all-done.qkv_ref), custom_call_target="tpu_custom_call" | custom-call | flops 9663676416 | bytes 4718592 | tf_op jit(solution)/shard_map/attend_own/pallas_call | solution.py:149
  85.8 1.2 copy-done.6
  86.9 14.9 %all-to-all-done.1 = bf16[256,16,128]{2,1,0:T(8,128)(2,1)S(1)} async-done(((bf16[256,16,128]{2,1,0:T(8,128)(2,1)}), bf16[256,16,128]{2,1,0:T(8,128)(2,1)S(1)}, u32[]{:S(2)}, u32[]{:S(2)}) %all-to-all-start.1) | async-done | bytes 1048608 | tf_op jit(solution)/shard_map/all_to_all | solution.py:233
  101.8 1.4 %copy-done.7 = f32[16,192,128]{2,1,0:T(8,128)S(1)} copy-done((f32[16,192,128]{2,1,0:T(8,128)S(1)}, f32[16,192,128]{2,1,0:T(8,128)}, u32[]{:S(2)}) %copy-start.7) | copy-done | bytes 1572888
  103.2 10.8 %attend_ref.1 = bf16[16,192,128]{2,1,0:T(8,128)(2,1)S(1)} custom-call(s32[1]{0:T(128)} %dynamic_slice.11.live_ref, bf16[16,3,192,128]{3,2,1,0:T(8,128)(2,1)S(1)} %all-to-all-done.qkv_ref, f32[16,192,128]{2,1,0:T(8,128)S(1)} %copy-done.7, f32[16,8,192]{2,1,0:T(8,128)S(1)} %get-tuple-element.34.stats_ref, bf16[8,2,16,16,128]{4,3,2,1,0:T(8,128)(2,1)S(1)} %bitcast.13), custom_call_target="tpu_custom_call" | custom-call | flops 6442450944 | bytes 6291456 | tf_op jit(solution)/shard_map/attend_ref/pallas_call | solution.py:214
  114.1 17.8 %all_to_all.15.x_ref = bf16[16,192,128]{2,1,0:T(8,128)(2,1)S(1)} all-to-all(bf16[16,192,128]{2,1,0:T(8,128)(2,1)S(1)} %attend_ref.1), channel_id=1, replica_groups=mesh['z'=8,'x'=2,'sp'=16] {'sp'}, dimensions={0} | all-to-all | bytes 1572864 | tf_op jit(solution)/shard_map/all_to_all | solution.py:233
  131.8 1.1 unpack_heads.1
  (17 shorter events, 0.0 us)
Async XLA Ops:
  1.1 14.3 %collective-permute-start = (bf16[128,2048]{1,0:T(8,128)(2,1)S(1)}, bf16[128,2048]{1,0:T(8,128)(2,1)S(1)}, u32[]{:S(2)}, u32[]{:S(2)}) collective-permute-start(bf16[128,2048]{1,0:T(8,128)(2,1)S(1)} %dynamic-slice_bitcast_fusion), channel_id=1, source_target_pairs={{0,16},{16,0},{1,17},{17,1},{2,18},{18,2},{3,19},{19,3},{4,20},{20... | collective-permute-start | bytes 1572872 | tf_op jit(solution)/shard_map/ppermute | solution.py:249
  4.7 1.1 copy-start.1
  5.9 1.1 copy-start.2
  7.0 1.1 copy-start.3
  8.1 7.2 %copy-start = (bf16[1,2,128,2048]{3,2,1,0:T(8,128)(2,1)S(1)}, bf16[1,2,128,2048]{3,2,1,0:T(8,128)(2,1)}, u32[]{:S(2)}) copy-start(bf16[1,2,128,2048]{3,2,1,0:T(8,128)(2,1)} %param.10) | copy-start | bytes 3145732
  16.0 39.0 %copy-start.4 = (s32[16]{0:T(128)S(1)}, s32[16]{0:T(128)}, u32[]{:S(2)}) copy-start(s32[16]{0:T(128)} %owner_ref.1) | copy-start | bytes 196
  16.0 39.0 %copy-start.5 = (s32[16]{0:T(128)S(1)}, s32[16]{0:T(128)}, u32[]{:S(2)}) copy-start(s32[16]{0:T(128)} %ids_ref.1) | copy-start | bytes 196
  16.0 40.9 %all-to-all-start = ((bf16[16,3,192,128]{3,2,1,0:T(8,128)(2,1)}), bf16[16,3,192,128]{3,2,1,0:T(8,128)(2,1)S(1)}, u32[]{:S(2)}, u32[]{:S(2)}) async-start(bf16[16,3,192,128]{3,2,1,0:T(8,128)(2,1)} %pack_heads.1), calls=%async_computation | async-start | bytes 4718592 | tf_op jit(solution)/shard_map/all_to_all | solution.py:233
  23.9 49.9 %copy-start.8 = (s32[16]{0:T(128)S(1)}, s32[16]{0:T(128)}, u32[]{:S(2)}) copy-start(s32[16]{0:T(128)} %param.13) | copy-start | bytes 196
  23.9 15.1 %collective-permute-start.1 = (bf16[2,16,2048]{2,1,0:T(8,128)(2,1)S(1)}, bf16[2,16,2048]{2,1,0:T(8,128)(2,1)S(1)}, u32[]{:S(2)}, u32[]{:S(2)}) collective-permute-start(bf16[2,16,2048]{2,1,0:T(8,128)(2,1)S(1)} %get-tuple-element.35), channel_id=1, source_target_pairs={{0,128},{32,160},{64,192},{96,224},{128,0},{160,32},{192,64},{224,... | collective-permute-start | bytes 393224 | tf_op jit(solution)/shard_map/ppermute | solution.py:239
  30.9 16.0 %collective-permute-start.2 = (bf16[2,16,2048]{2,1,0:T(8,128)(2,1)S(1)}, bf16[2,16,2048]{2,1,0:T(8,128)(2,1)S(1)}, u32[]{:S(2)}, u32[]{:S(2)}) collective-permute-start(bf16[2,16,2048]{2,1,0:T(8,128)(2,1)S(1)} %get-tuple-element.36), channel_id=1, source_target_pairs={{0,96},{32,128},{64,160},{96,192},{128,224},{160,0},{192,32},{224,... | collective-permute-start | bytes 393224 | tf_op jit(solution)/shard_map/ppermute | solution.py:239
  32.6 14.4 %collective-permute-start.3 = (bf16[2,16,2048]{2,1,0:T(8,128)(2,1)S(1)}, bf16[2,16,2048]{2,1,0:T(8,128)(2,1)S(1)}, u32[]{:S(2)}, u32[]{:S(2)}) collective-permute-start(bf16[2,16,2048]{2,1,0:T(8,128)(2,1)S(1)} %get-tuple-element.37), channel_id=1, source_target_pairs={{0,160},{32,192},{64,224},{96,0},{128,32},{160,64},{192,96},{224,1... | collective-permute-start | bytes 393224 | tf_op jit(solution)/shard_map/ppermute | solution.py:239
  35.4 12.8 %collective-permute-start.4 = (bf16[2,16,2048]{2,1,0:T(8,128)(2,1)S(1)}, bf16[2,16,2048]{2,1,0:T(8,128)(2,1)S(1)}, u32[]{:S(2)}, u32[]{:S(2)}) collective-permute-start(bf16[2,16,2048]{2,1,0:T(8,128)(2,1)S(1)} %get-tuple-element.38), channel_id=1, source_target_pairs={{0,64},{32,96},{64,128},{96,160},{128,192},{160,224},{192,0},{224,... | collective-permute-start | bytes 393224 | tf_op jit(solution)/shard_map/ppermute | solution.py:239
  36.6 15.0 %collective-permute-start.5 = (bf16[2,16,2048]{2,1,0:T(8,128)(2,1)S(1)}, bf16[2,16,2048]{2,1,0:T(8,128)(2,1)S(1)}, u32[]{:S(2)}, u32[]{:S(2)}) collective-permute-start(bf16[2,16,2048]{2,1,0:T(8,128)(2,1)S(1)} %get-tuple-element.39), channel_id=1, source_target_pairs={{0,192},{32,224},{64,0},{96,32},{128,64},{160,96},{192,128},{224,1... | collective-permute-start | bytes 393224 | tf_op jit(solution)/shard_map/ppermute | solution.py:239
  39.0 15.3 %collective-permute-start.6 = (bf16[2,16,2048]{2,1,0:T(8,128)(2,1)S(1)}, bf16[2,16,2048]{2,1,0:T(8,128)(2,1)S(1)}, u32[]{:S(2)}, u32[]{:S(2)}) collective-permute-start(bf16[2,16,2048]{2,1,0:T(8,128)(2,1)S(1)} %get-tuple-element.40), channel_id=1, source_target_pairs={{0,32},{32,64},{64,96},{96,128},{128,160},{160,192},{192,224},{224... | collective-permute-start | bytes 393224 | tf_op jit(solution)/shard_map/ppermute | solution.py:239
  47.0 8.0 %collective-permute-start.7 = (bf16[2,16,2048]{2,1,0:T(8,128)(2,1)S(1)}, bf16[2,16,2048]{2,1,0:T(8,128)(2,1)S(1)}, u32[]{:S(2)}, u32[]{:S(2)}) collective-permute-start(bf16[2,16,2048]{2,1,0:T(8,128)(2,1)S(1)} %get-tuple-element.41), channel_id=1, source_target_pairs={{0,224},{32,0},{64,32},{96,64},{128,96},{160,128},{192,160},{224,1... | collective-permute-start | bytes 393224 | tf_op jit(solution)/shard_map/ppermute | solution.py:239
  56.9 44.9 %all-to-all-start.1 = ((bf16[256,16,128]{2,1,0:T(8,128)(2,1)}), bf16[256,16,128]{2,1,0:T(8,128)(2,1)S(1)}, u32[]{:S(2)}, u32[]{:S(2)}) async-start(bf16[256,16,128]{2,1,0:T(8,128)(2,1)} %bitcast.8), calls=%async_computation.1 | async-start | bytes 2097152 | tf_op jit(solution)/shard_map/all_to_all | solution.py:233
  85.8 1.2 copy-start.6
  101.8 1.4 %copy-start.7 = (f32[16,192,128]{2,1,0:T(8,128)S(1)}, f32[16,192,128]{2,1,0:T(8,128)}, u32[]{:S(2)}) copy-start(f32[16,192,128]{2,1,0:T(8,128)} %copy-done.6) | copy-start | bytes 4718596

commit v4 on v3

--- a/solution.py
+++ b/solution.py
@@ -212,8 +212,8 @@
     n = shards * tokens
     n_keys = kv.size // (2 * D)
     return pl.pallas_call(
-        functools.partial(ref_kernel, per_row=PER_ROW, steps=2),
-        grid=(shards // PER_ROW,),
+        functools.partial(ref_kernel, per_row=shards, steps=1),
+        grid=(1,),
         in_specs=[whole(pltpu.SMEM)] + [whole()] * 4,
         out_specs=whole(),
         out_shape=jax.ShapeDtypeStruct((shards, tokens, D), jnp.bfloat16),

time: 134 us -> 132 us (0.985)
  transfers between devices with their start and end apart: 10 -> 10, of which waited for: 7 -> 7; matrix products, arithmetic and copies ran while one was open for 1% -> 1% of each run, Pallas kernels for 11% -> 12%
where the time goes in v4:
time: 132 us
  starting transfers between devices  41.8 us (32%)
  waiting for transfers between devices  35.3 us (27%)
  Pallas kernels  26.5 us (20%)
  blocking collectives  17.8 us (13%)
  local copies, waits for them, and re-layouts  8.24 us (6%)
  between operations  2.03 us (2%)
    all_to_all x2, starting transfers between devices, swap(): return lax.all_to_all(x, axes, split_axis=0, concat_axis=0, tiled=True)  22.3 us
    all_to_all x1, blocking collectives, swap(): return lax.all_to_all(x, axes, split_axis=0, concat_axis=0, tiled=True)  17.8 us
    ppermute x7, starting transfers between devices, shift_z(): lax.ppermute(piece, 'z', [(src, (src + shift) % n_z) for src in range(n_z)])  15.8 us
    ppermute x7, waiting for transfers between devices, shift_z(): lax.ppermute(piece, 'z', [(src, (src + shift) % n_z) for src in range(n_z)])  15.2 us
    all_to_all x2, waiting for transfers between devices, swap(): return lax.all_to_all(x, axes, split_axis=0, concat_axis=0, tiled=True)  14.9 us
    pallas_call x1, Pallas kernels, attend_own(): pl.pallas_call(functools.partial(own_kernel, per_row=PER_ROW, steps=4), g...  11.4 us
    pallas_call x1, Pallas kernels, attend_ref(): pl.pallas_call(functools.partial(ref_kernel, per_row=shards, steps=1), gr...  9.62 us
    unnamed x18, local copies, waits for them, and re-layouts  6 us
  transfers between devices with their start and end apart: 10, of which 7 were waited for; matrix products, arithmetic and copies ran while one was open for 1% of the time, Pallas kernels for 12%

profile of v4, /device:TPU:1, one launch (start us, length us, event | category | flops | bytes accessed | tf_op | source)
XLA Modules:
  0.0 131.7 jit_solution(16550615107120762893)
XLA Ops:
  0.0 1.1 dynamic-slice_bitcast_fusion
  1.1 3.7 %collective-permute-start = (bf16[128,2048]{1,0:T(8,128)(2,1)S(1)}, bf16[128,2048]{1,0:T(8,128)(2,1)S(1)}, u32[]{:S(2)}, u32[]{:S(2)}) collective-permute-start(bf16[128,2048]{1,0:T(8,128)(2,1)S(1)} %dynamic-slice_bitcast_fusion), channel_id=1, source_target_pairs={{0,16},{16,0},{1,17},{17,1},{2,18},{18,2},{3,19},{19,3},{4,20},{20... | collective-permute-start | bytes 1572872 | tf_op jit(solution)/shard_map/ppermute | solution.py:249
  4.7 1.1 copy-done.1
  5.9 1.1 copy-done.2
  7.0 1.1 copy-done.3
  8.1 1.9 %pack_heads.1 = bf16[16,3,192,128]{3,2,1,0:T(8,128)(2,1)} custom-call(bf16[192,2048]{1,0:T(8,128)(2,1)S(1)} %bitcast.14, bf16[192,2048]{1,0:T(8,128)(2,1)S(1)} %bitcast.15, bf16[192,2048]{1,0:T(8,128)(2,1)S(1)} %bitcast.16), custom_call_target="tpu_custom_call" | custom-call | bytes 4718592 | tf_op jit(solution)/shard_map/pack_heads/pallas_call | solution.py:36
  10.0 0.1 pad_add_fusion.place_ref
  10.1 5.2 %collective-permute-done.other_ref = bf16[128,2048]{1,0:T(8,128)(2,1)S(1)} collective-permute-done((bf16[128,2048]{1,0:T(8,128)(2,1)S(1)}, bf16[128,2048]{1,0:T(8,128)(2,1)S(1)}, u32[]{:S(2)}, u32[]{:S(2)}) %collective-permute-start) | collective-permute-done | bytes 524320 | tf_op jit(solution)/shard_map/ppermute | solution.py:249
  15.3 0.6 spread_pieces.1
  16.0 7.9 %all-to-all-start = ((bf16[16,3,192,128]{3,2,1,0:T(8,128)(2,1)}), bf16[16,3,192,128]{3,2,1,0:T(8,128)(2,1)S(1)}, u32[]{:S(2)}, u32[]{:S(2)}) async-start(bf16[16,3,192,128]{3,2,1,0:T(8,128)(2,1)} %pack_heads.1), calls=%async_computation | async-start | bytes 4718592 | tf_op jit(solution)/shard_map/all_to_all | solution.py:233
  23.9 7.0 %collective-permute-start.1 = (bf16[2,16,2048]{2,1,0:T(8,128)(2,1)S(1)}, bf16[2,16,2048]{2,1,0:T(8,128)(2,1)S(1)}, u32[]{:S(2)}, u32[]{:S(2)}) collective-permute-start(bf16[2,16,2048]{2,1,0:T(8,128)(2,1)S(1)} %get-tuple-element.35), channel_id=1, source_target_pairs={{0,128},{32,160},{64,192},{96,224},{128,0},{160,32},{192,64},{224,... | collective-permute-start | bytes 393224 | tf_op jit(solution)/shard_map/ppermute | solution.py:239
  30.9 1.6 %collective-permute-start.2 = (bf16[2,16,2048]{2,1,0:T(8,128)(2,1)S(1)}, bf16[2,16,2048]{2,1,0:T(8,128)(2,1)S(1)}, u32[]{:S(2)}, u32[]{:S(2)}) collective-permute-start(bf16[2,16,2048]{2,1,0:T(8,128)(2,1)S(1)} %get-tuple-element.36), channel_id=1, source_target_pairs={{0,96},{32,128},{64,160},{96,192},{128,224},{160,0},{192,32},{224,... | collective-permute-start | bytes 393224 | tf_op jit(solution)/shard_map/ppermute | solution.py:239
  32.6 2.8 %collective-permute-start.3 = (bf16[2,16,2048]{2,1,0:T(8,128)(2,1)S(1)}, bf16[2,16,2048]{2,1,0:T(8,128)(2,1)S(1)}, u32[]{:S(2)}, u32[]{:S(2)}) collective-permute-start(bf16[2,16,2048]{2,1,0:T(8,128)(2,1)S(1)} %get-tuple-element.37), channel_id=1, source_target_pairs={{0,160},{32,192},{64,224},{96,0},{128,32},{160,64},{192,96},{224,1... | collective-permute-start | bytes 393224 | tf_op jit(solution)/shard_map/ppermute | solution.py:239
  35.4 1.2 collective-permute-start.4
  36.6 2.4 %collective-permute-start.5 = (bf16[2,16,2048]{2,1,0:T(8,128)(2,1)S(1)}, bf16[2,16,2048]{2,1,0:T(8,128)(2,1)S(1)}, u32[]{:S(2)}, u32[]{:S(2)}) collective-permute-start(bf16[2,16,2048]{2,1,0:T(8,128)(2,1)S(1)} %get-tuple-element.39), channel_id=1, source_target_pairs={{0,192},{32,224},{64,0},{96,32},{128,64},{160,96},{192,128},{224,1... | collective-permute-start | bytes 393224 | tf_op jit(solution)/shard_map/ppermute | solution.py:239
  39.0 0.7 collective-permute-start.6
  39.7 7.2 %collective-permute-done.2.refs_1_ = bf16[2,16,2048]{2,1,0:T(8,128)(2,1)S(1)} collective-permute-done((bf16[2,16,2048]{2,1,0:T(8,128)(2,1)S(1)}, bf16[2,16,2048]{2,1,0:T(8,128)(2,1)S(1)}, u32[]{:S(2)}, u32[]{:S(2)}) %collective-permute-start.2) | collective-permute-done | bytes 131104 | tf_op jit(solution)/shard_map/ppermute | solution.py:239
  47.0 1.3 collective-permute-done.4.refs_3_
  48.2 3.3 %collective-permute-done.5.refs_4_ = bf16[2,16,2048]{2,1,0:T(8,128)(2,1)S(1)} collective-permute-done((bf16[2,16,2048]{2,1,0:T(8,128)(2,1)S(1)}, bf16[2,16,2048]{2,1,0:T(8,128)(2,1)S(1)}, u32[]{:S(2)}, u32[]{:S(2)}) %collective-permute-start.5) | collective-permute-done | bytes 131104 | tf_op jit(solution)/shard_map/ppermute | solution.py:239
  51.6 2.7 %collective-permute-done.6.refs_5_ = bf16[2,16,2048]{2,1,0:T(8,128)(2,1)S(1)} collective-permute-done((bf16[2,16,2048]{2,1,0:T(8,128)(2,1)S(1)}, bf16[2,16,2048]{2,1,0:T(8,128)(2,1)S(1)}, u32[]{:S(2)}, u32[]{:S(2)}) %collective-permute-start.6) | collective-permute-done | bytes 131104 | tf_op jit(solution)/shard_map/ppermute | solution.py:239
  54.3 0.7 collective-permute-done.7.refs_6_
  55.0 1.9 %route_pieces.1 = bf16[16,16,16,128]{3,2,1,0:T(8,128)(2,1)} custom-call(s32[2]{0:T(128)S(1)} %pad_add_fusion.place_ref, s32[16]{0:T(128)S(1)} %copy-done.5, s32[16]{0:T(128)S(1)} %copy-done.4, bf16[2,16,2048]{2,1,0:T(8,128)(2,1)S(1)} %collective-permute-done.1.refs_0_, bf16[2,16,2048]{2,1,0:T(8,128)(2,1)S(1)} %collective-permute-done.2.refs_1_, ...), custom_call_target="tpu_custom_call" | custom-call | bytes 2097152 | tf_op jit(solution)/shard_map/route_pieces/pallas_call | solution.py:84
  56.9 14.4 %all-to-all-start.1 = ((bf16[256,16,128]{2,1,0:T(8,128)(2,1)}), bf16[256,16,128]{2,1,0:T(8,128)(2,1)S(1)}, u32[]{:S(2)}, u32[]{:S(2)}) async-start(bf16[256,16,128]{2,1,0:T(8,128)(2,1)} %bitcast.8), calls=%async_computation.1 | async-start | bytes 2097152 | tf_op jit(solution)/shard_map/all_to_all | solution.py:233
  71.2 0.6 dynamic_slice.10
  73.8 0.6 dynamic_slice.11.live_ref
  74.4 11.4 %attend_own.1 = (f32[16,192,128]{2,1,0:T(8,128)S(1)}, f32[16,8,192]{2,1,0:T(8,128)S(1)}) custom-call(bf16[16,3,192,128]{3,2,1,0:T(8,128)(2,1)S(1)} %all-to-all-done.qkv_ref), custom_call_target="tpu_custom_call" | custom-call | flops 9663676416 | bytes 4718592 | tf_op jit(solution)/shard_map/attend_own/pallas_call | solution.py:149
  85.8 1.2 copy-done.6
  86.9 14.9 %all-to-all-done.1 = bf16[256,16,128]{2,1,0:T(8,128)(2,1)S(1)} async-done(((bf16[256,16,128]{2,1,0:T(8,128)(2,1)}), bf16[256,16,128]{2,1,0:T(8,128)(2,1)S(1)}, u32[]{:S(2)}, u32[]{:S(2)}) %all-to-all-start.1) | async-done | bytes 1048608 | tf_op jit(solution)/shard_map/all_to_all | solution.py:233
  101.8 1.4 %copy-done.7 = f32[16,192,128]{2,1,0:T(8,128)S(1)} copy-done((f32[16,192,128]{2,1,0:T(8,128)S(1)}, f32[16,192,128]{2,1,0:T(8,128)}, u32[]{:S(2)}) %copy-start.7) | copy-done | bytes 1572888
  103.2 9.6 %attend_ref.1 = bf16[16,192,128]{2,1,0:T(8,128)(2,1)S(1)} custom-call(s32[1]{0:T(128)} %dynamic_slice.11.live_ref, bf16[16,3,192,128]{3,2,1,0:T(8,128)(2,1)S(1)} %all-to-all-done.qkv_ref, f32[16,192,128]{2,1,0:T(8,128)S(1)} %copy-done.7, f32[16,8,192]{2,1,0:T(8,128)S(1)} %get-tuple-element.34.stats_ref, bf16[8,2,16,16,128]{4,3,2,1,0:T(8,128)(2,1)S(1)} %bitcast.13), custom_call_target="tpu_custom_call" | custom-call | flops 6442450944 | bytes 6291456 | tf_op jit(solution)/shard_map/attend_ref/pallas_call | solution.py:214
  112.8 17.8 %all_to_all.15.x_ref = bf16[16,192,128]{2,1,0:T(8,128)(2,1)S(1)} all-to-all(bf16[16,192,128]{2,1,0:T(8,128)(2,1)S(1)} %attend_ref.1), channel_id=1, replica_groups=mesh['z'=8,'x'=2,'sp'=16] {'sp'}, dimensions={0} | all-to-all | bytes 1572864 | tf_op jit(solution)/shard_map/all_to_all | solution.py:233
  130.6 1.1 unpack_heads.1
  (17 shorter events, 0.0 us)
Async XLA Ops:
  1.1 14.3 %collective-permute-start = (bf16[128,2048]{1,0:T(8,128)(2,1)S(1)}, bf16[128,2048]{1,0:T(8,128)(2,1)S(1)}, u32[]{:S(2)}, u32[]{:S(2)}) collective-permute-start(bf16[128,2048]{1,0:T(8,128)(2,1)S(1)} %dynamic-slice_bitcast_fusion), channel_id=1, source_target_pairs={{0,16},{16,0},{1,17},{17,1},{2,18},{18,2},{3,19},{19,3},{4,20},{20... | collective-permute-start | bytes 1572872 | tf_op jit(solution)/shard_map/ppermute | solution.py:249
  4.7 1.1 copy-start.1
  5.9 1.1 copy-start.2
  7.0 1.1 copy-start.3
  8.1 7.2 %copy-start = (bf16[1,2,128,2048]{3,2,1,0:T(8,128)(2,1)S(1)}, bf16[1,2,128,2048]{3,2,1,0:T(8,128)(2,1)}, u32[]{:S(2)}) copy-start(bf16[1,2,128,2048]{3,2,1,0:T(8,128)(2,1)} %param.10) | copy-start | bytes 3145732
  16.0 39.0 %copy-start.4 = (s32[16]{0:T(128)S(1)}, s32[16]{0:T(128)}, u32[]{:S(2)}) copy-start(s32[16]{0:T(128)} %owner_ref.1) | copy-start | bytes 196
  16.0 39.0 %copy-start.5 = (s32[16]{0:T(128)S(1)}, s32[16]{0:T(128)}, u32[]{:S(2)}) copy-start(s32[16]{0:T(128)} %ids_ref.1) | copy-start | bytes 196
  16.0 40.9 %all-to-all-start = ((bf16[16,3,192,128]{3,2,1,0:T(8,128)(2,1)}), bf16[16,3,192,128]{3,2,1,0:T(8,128)(2,1)S(1)}, u32[]{:S(2)}, u32[]{:S(2)}) async-start(bf16[16,3,192,128]{3,2,1,0:T(8,128)(2,1)} %pack_heads.1), calls=%async_computation | async-start | bytes 4718592 | tf_op jit(solution)/shard_map/all_to_all | solution.py:233
  23.9 49.9 %copy-start.8 = (s32[16]{0:T(128)S(1)}, s32[16]{0:T(128)}, u32[]{:S(2)}) copy-start(s32[16]{0:T(128)} %param.13) | copy-start | bytes 196
  23.9 15.1 %collective-permute-start.1 = (bf16[2,16,2048]{2,1,0:T(8,128)(2,1)S(1)}, bf16[2,16,2048]{2,1,0:T(8,128)(2,1)S(1)}, u32[]{:S(2)}, u32[]{:S(2)}) collective-permute-start(bf16[2,16,2048]{2,1,0:T(8,128)(2,1)S(1)} %get-tuple-element.35), channel_id=1, source_target_pairs={{0,128},{32,160},{64,192},{96,224},{128,0},{160,32},{192,64},{224,... | collective-permute-start | bytes 393224 | tf_op jit(solution)/shard_map/ppermute | solution.py:239
  30.9 16.0 %collective-permute-start.2 = (bf16[2,16,2048]{2,1,0:T(8,128)(2,1)S(1)}, bf16[2,16,2048]{2,1,0:T(8,128)(2,1)S(1)}, u32[]{:S(2)}, u32[]{:S(2)}) collective-permute-start(bf16[2,16,2048]{2,1,0:T(8,128)(2,1)S(1)} %get-tuple-element.36), channel_id=1, source_target_pairs={{0,96},{32,128},{64,160},{96,192},{128,224},{160,0},{192,32},{224,... | collective-permute-start | bytes 393224 | tf_op jit(solution)/shard_map/ppermute | solution.py:239
  32.6 14.4 %collective-permute-start.3 = (bf16[2,16,2048]{2,1,0:T(8,128)(2,1)S(1)}, bf16[2,16,2048]{2,1,0:T(8,128)(2,1)S(1)}, u32[]{:S(2)}, u32[]{:S(2)}) collective-permute-start(bf16[2,16,2048]{2,1,0:T(8,128)(2,1)S(1)} %get-tuple-element.37), channel_id=1, source_target_pairs={{0,160},{32,192},{64,224},{96,0},{128,32},{160,64},{192,96},{224,1... | collective-permute-start | bytes 393224 | tf_op jit(solution)/shard_map/ppermute | solution.py:239
  35.4 12.8 %collective-permute-start.4 = (bf16[2,16,2048]{2,1,0:T(8,128)(2,1)S(1)}, bf16[2,16,2048]{2,1,0:T(8,128)(2,1)S(1)}, u32[]{:S(2)}, u32[]{:S(2)}) collective-permute-start(bf16[2,16,2048]{2,1,0:T(8,128)(2,1)S(1)} %get-tuple-element.38), channel_id=1, source_target_pairs={{0,64},{32,96},{64,128},{96,160},{128,192},{160,224},{192,0},{224,... | collective-permute-start | bytes 393224 | tf_op jit(solution)/shard_map/ppermute | solution.py:239
  36.6 15.0 %collective-permute-start.5 = (bf16[2,16,2048]{2,1,0:T(8,128)(2,1)S(1)}, bf16[2,16,2048]{2,1,0:T(8,128)(2,1)S(1)}, u32[]{:S(2)}, u32[]{:S(2)}) collective-permute-start(bf16[2,16,2048]{2,1,0:T(8,128)(2,1)S(1)} %get-tuple-element.39), channel_id=1, source_target_pairs={{0,192},{32,224},{64,0},{96,32},{128,64},{160,96},{192,128},{224,1... | collective-permute-start | bytes 393224 | tf_op jit(solution)/shard_map/ppermute | solution.py:239
  39.0 15.3 %collective-permute-start.6 = (bf16[2,16,2048]{2,1,0:T(8,128)(2,1)S(1)}, bf16[2,16,2048]{2,1,0:T(8,128)(2,1)S(1)}, u32[]{:S(2)}, u32[]{:S(2)}) collective-permute-start(bf16[2,16,2048]{2,1,0:T(8,128)(2,1)S(1)} %get-tuple-element.40), channel_id=1, source_target_pairs={{0,32},{32,64},{64,96},{96,128},{128,160},{160,192},{192,224},{224... | collective-permute-start | bytes 393224 | tf_op jit(solution)/shard_map/ppermute | solution.py:239
  47.0 8.0 %collective-permute-start.7 = (bf16[2,16,2048]{2,1,0:T(8,128)(2,1)S(1)}, bf16[2,16,2048]{2,1,0:T(8,128)(2,1)S(1)}, u32[]{:S(2)}, u32[]{:S(2)}) collective-permute-start(bf16[2,16,2048]{2,1,0:T(8,128)(2,1)S(1)} %get-tuple-element.41), channel_id=1, source_target_pairs={{0,224},{32,0},{64,32},{96,64},{128,96},{160,128},{192,160},{224,1... | collective-permute-start | bytes 393224 | tf_op jit(solution)/shard_map/ppermute | solution.py:239
  56.9 44.9 %all-to-all-start.1 = ((bf16[256,16,128]{2,1,0:T(8,128)(2,1)}), bf16[256,16,128]{2,1,0:T(8,128)(2,1)S(1)}, u32[]{:S(2)}, u32[]{:S(2)}) async-start(bf16[256,16,128]{2,1,0:T(8,128)(2,1)} %bitcast.8), calls=%async_computation.1 | async-start | bytes 2097152 | tf_op jit(solution)/shard_map/all_to_all | solution.py:233
  85.8 1.2 copy-start.6
  101.8 1.4 %copy-start.7 = (f32[16,192,128]{2,1,0:T(8,128)S(1)}, f32[16,192,128]{2,1,0:T(8,128)}, u32[]{:S(2)}) copy-start(f32[16,192,128]{2,1,0:T(8,128)} %copy-done.6) | copy-start | bytes 4718596

commit v5 on v4

--- a/solution.py
+++ b/solution.py
@@ -124,23 +124,36 @@
     return part, peak
 
 
-def own_kernel(qkv_ref, acc_ref, stats_ref, *, per_row, steps):
+def own_kernel(qkv_ref, out_ref, stats_ref, means, *, per_row, steps):
     shards, _, tokens, _ = qkv_ref.shape
     per = shards // steps
-    base = pl.program_id(0) * per_row
-    for i in range(per_row):
-        q = qkv_ref[base + i, 0]
-        state = None
-        for step in range(steps):
-            here = slice(step * per, (step + 1) * per)
-            k = qkv_ref[here, 1].reshape(per * tokens, D)
-            v = qkv_ref[here, 2].reshape(per * tokens, D)
-            v_ones = jnp.concatenate([v, jnp.ones_like(v)], axis=1)
-            state = attend_block(q, k, v_ones, state)
-        acc_ref[base + i] = state[0][:, :D]
-        column = lax.broadcasted_iota(jnp.int32, (tokens, D), 1)
-        stats = jnp.where(column == 0, state[0][:, D:], state[1])
-        stats_ref[base + i] = jnp.transpose(stats)[: stats_ref.shape[1]]
+    row, rows = pl.program_id(0), shards // per_row
+
+    @pl.when(row < rows)
+    def _():
+        base = row * per_row
+        for i in range(per_row):
+            q = qkv_ref[base + i, 0]
+            state = None
+            for step in range(steps):
+                here = slice(step * per, (step + 1) * per)
+                k = qkv_ref[here, 1].reshape(per * tokens, D)
+                v = qkv_ref[here, 2].reshape(per * tokens, D)
+                v_ones = jnp.concatenate([v, jnp.ones_like(v)], axis=1)
+                state = attend_block(q, k, v_ones, state)
+            mean = state[0][:, :D] / state[0][:, D:]
+            high = mean.astype(jnp.bfloat16)
+            means[base + i, 0] = high
+            means[base + i, 1] = (mean - high.astype(jnp.float32)).astype(jnp.bfloat16)
+            column = lax.broadcasted_iota(jnp.int32, (tokens, D), 1)
+            stats = jnp.where(column == 0, state[0][:, D:], state[1])
+            stats_ref[base + i] = jnp.transpose(stats)[: stats_ref.shape[1]]
+
+    @pl.when(row == rows)
+    def _():
+        out_ref[:, 0] = qkv_ref[:, 0]
+        out_ref[:, 1] = means[:, 0]
+        out_ref[:, 2] = means[:, 1]
 
 
 def attend_own(qkv):
@@ -148,13 +161,15 @@
     n = shards * tokens
     return pl.pallas_call(
         functools.partial(own_kernel, per_row=PER_ROW, steps=4),
-        grid=(shards // PER_ROW,),
+        grid=(shards // PER_ROW + 1,),
         in_specs=[whole()],
         out_specs=[whole()] * 2,
         out_shape=[
-            jax.ShapeDtypeStruct((shards, tokens, D), jnp.float32),
+            jax.ShapeDtypeStruct(qkv.shape, qkv.dtype),
             jax.ShapeDtypeStruct((shards, 8, tokens), jnp.float32),
         ],
+        scratch_shapes=[pltpu.VMEM((shards, 2, tokens, D), jnp.bfloat16)],
+        input_output_aliases={0: 0},
         compiler_params=params(),
         cost_estimate=pl.CostEstimate(
             flops=8 * n * n * D, bytes_accessed=12 * n * D, transcendentals=n * n
@@ -164,7 +179,7 @@
 
 
 def ref_kernel(
-    live_ref, qkv_ref, acc_ref, stats_ref, kv_ref, out_ref, k_held, v_held, *, per_row, steps
+    live_ref, own_ref, stats_ref, kv_ref, out_ref, k_held, v_held, *, per_row, steps
 ):
     pieces, _, shards, tokens, _ = kv_ref.shape
     n_keys = pieces * shards * tokens
@@ -193,28 +208,29 @@
                 v_held[keys, D:] = jnp.where(live, 1.0, 0.0).astype(jnp.bfloat16)
 
     base = pl.program_id(0) * per_row
-    rows = qkv_ref.shape[2]
+    rows = own_ref.shape[2]
     for i in range(per_row):
-        q = qkv_ref[base + i, 0]
+        q = own_ref[base + i, 0]
         stats = stats_ref[base + i]
         total, peak = (
             jnp.transpose(jnp.broadcast_to(stats[j : j + 1], (D, rows))) for j in range(2)
         )
-        state = (jnp.concatenate([acc_ref[base + i], total], axis=1), peak[:, :1])
+        high, low = (own_ref[base + i, j].astype(jnp.float32) for j in (1, 2))
+        state = (jnp.concatenate([(high + low) * total, total], axis=1), peak[:, :1])
         for step in range(steps):
             keys = slice(step * block, (step + 1) * block)
             state = attend_block(q, k_held[keys], v_held[keys], state)
         out_ref[base + i] = (state[0][:, :D] / state[0][:, D:]).astype(jnp.bfloat16)
 
 
-def attend_ref(qkv, acc, stats, kv, live):
-    shards, _, tokens, _ = qkv.shape
+def attend_ref(own, stats, kv, live):
+    shards, _, tokens, _ = own.shape
     n = shards * tokens
     n_keys = kv.size // (2 * D)
     return pl.pallas_call(
         functools.partial(ref_kernel, per_row=shards, steps=1),
         grid=(1,),
-        in_specs=[whole(pltpu.SMEM)] + [whole()] * 4,
+        in_specs=[whole(pltpu.SMEM)] + [whole()] * 3,
         out_specs=whole(),
         out_shape=jax.ShapeDtypeStruct((shards, tokens, D), jnp.bfloat16),
         scratch_shapes=[
@@ -226,7 +242,7 @@
             flops=8 * n * n_keys * D, bytes_accessed=16 * n * D, transcendentals=n * n_keys
         ),
         name="attend_ref",
-    )(live, qkv, acc, stats, kv)
+    )(live, own, stats, kv)
 
 
 def swap(x, axes):
@@ -260,7 +276,7 @@
     tokens = routed.shape[2]
     kv = swap(routed.reshape(-1, tokens, D), ("z", "x", "sp")).reshape(n_z, 2, -1, tokens, D)
 
-    out = attend_ref(qkv, *attend_own(qkv), kv, live)
+    out = attend_ref(*attend_own(qkv), kv, live)
 
     back = swap(out, "sp")
     return unpack_heads(back)[None]

time: 132 us -> 131 us (level)
  local copies, waits for them, and re-layouts: 8.24 us -> 5.67 us
    unnamed x18 -> x14, local copies, waits for them, and re-layouts: 6 us -> 3.42 us
where the time goes in v5:
time: 131 us; the launch traced here: 130 us
  starting transfers between devices  41.8 us (32%)
  waiting for transfers between devices  36.3 us (28%)
  Pallas kernels  26.8 us (20%)
  blocking collectives  17.8 us (14%)
  local copies, waits for them, and re-layouts  5.67 us (4%)
  between operations  2.03 us (2%)
    all_to_all x2, starting transfers between devices, swap(): return lax.all_to_all(x, axes, split_axis=0, concat_axis=0, tiled=True)  22.3 us
    all_to_all x1, blocking collectives, swap(): return lax.all_to_all(x, axes, split_axis=0, concat_axis=0, tiled=True)  17.8 us
    all_to_all x2, waiting for transfers between devices, swap(): return lax.all_to_all(x, axes, split_axis=0, concat_axis=0, tiled=True)  15.8 us
    ppermute x7, starting transfers between devices, shift_z(): lax.ppermute(piece, 'z', [(src, (src + shift) % n_z) for src in range(n_z)])  15.8 us
    ppermute x7, waiting for transfers between devices, shift_z(): lax.ppermute(piece, 'z', [(src, (src + shift) % n_z) for src in range(n_z)])  15.2 us
    pallas_call x1, Pallas kernels, attend_own(): pl.pallas_call(functools.partial(own_kernel, per_row=PER_ROW, steps=4), g...  11.6 us
    pallas_call x1, Pallas kernels, attend_ref(): pl.pallas_call(functools.partial(ref_kernel, per_row=shards, steps=1), gr...  9.7 us
    ppermute x1, waiting for transfers between devices, shards(): other = lax.ppermute(other, 'x', [(0, 1), (1, 0)])  5.27 us
  transfers between devices with their start and end apart: 10, of which 7 were waited for; matrix products, arithmetic and copies ran while one was open for 1% of the time, Pallas kernels for 12%

profile of v5, /device:TPU:1, one launch (start us, length us, event | category | flops | bytes accessed | tf_op | source)
XLA Modules:
  0.0 130.4 jit_solution(13098157129075119699)
XLA Ops:
  0.0 1.1 dynamic-slice_bitcast_fusion
  1.1 3.7 %collective-permute-start = (bf16[128,2048]{1,0:T(8,128)(2,1)S(1)}, bf16[128,2048]{1,0:T(8,128)(2,1)S(1)}, u32[]{:S(2)}, u32[]{:S(2)}) collective-permute-start(bf16[128,2048]{1,0:T(8,128)(2,1)S(1)} %dynamic-slice_bitcast_fusion), channel_id=1, source_target_pairs={{0,16},{16,0},{1,17},{17,1},{2,18},{18,2},{3,19},{19,3},{4,20},{20... | collective-permute-start | bytes 1572872 | tf_op jit(solution)/shard_map/ppermute | solution.py:265
  4.7 1.1 copy-done.1
  5.9 1.1 copy-done.2
  7.0 1.1 copy-done.3
  8.1 1.8 %pack_heads.1 = bf16[16,3,192,128]{3,2,1,0:T(8,128)(2,1)} custom-call(bf16[192,2048]{1,0:T(8,128)(2,1)S(1)} %bitcast.14, bf16[192,2048]{1,0:T(8,128)(2,1)S(1)} %bitcast.15, bf16[192,2048]{1,0:T(8,128)(2,1)S(1)} %bitcast.16), custom_call_target="tpu_custom_call" | custom-call | bytes 4718592 | tf_op jit(solution)/shard_map/pack_heads/pallas_call | solution.py:36
  10.0 0.1 pad_add_fusion.place_ref
  10.1 5.3 %collective-permute-done.other_ref = bf16[128,2048]{1,0:T(8,128)(2,1)S(1)} collective-permute-done((bf16[128,2048]{1,0:T(8,128)(2,1)S(1)}, bf16[128,2048]{1,0:T(8,128)(2,1)S(1)}, u32[]{:S(2)}, u32[]{:S(2)}) %collective-permute-start) | collective-permute-done | bytes 524320 | tf_op jit(solution)/shard_map/ppermute | solution.py:265
  15.3 0.6 spread_pieces.1
  16.0 0.0 copy-start.4
  16.0 0.0 copy-start.5
  16.0 7.9 %all-to-all-start = ((bf16[16,3,192,128]{3,2,1,0:T(8,128)(2,1)}), bf16[16,3,192,128]{3,2,1,0:T(8,128)(2,1)S(1)}, u32[]{:S(2)}, u32[]{:S(2)}) async-start(bf16[16,3,192,128]{3,2,1,0:T(8,128)(2,1)} %pack_heads.1), calls=%async_computation | async-start | bytes 4718592 | tf_op jit(solution)/shard_map/all_to_all | solution.py:249
  23.9 7.0 %collective-permute-start.1 = (bf16[2,16,2048]{2,1,0:T(8,128)(2,1)S(1)}, bf16[2,16,2048]{2,1,0:T(8,128)(2,1)S(1)}, u32[]{:S(2)}, u32[]{:S(2)}) collective-permute-start(bf16[2,16,2048]{2,1,0:T(8,128)(2,1)S(1)} %get-tuple-element.35), channel_id=1, source_target_pairs={{0,128},{32,160},{64,192},{96,224},{128,0},{160,32},{192,64},{224,... | collective-permute-start | bytes 393224 | tf_op jit(solution)/shard_map/ppermute | solution.py:255
  30.9 1.6 %collective-permute-start.2 = (bf16[2,16,2048]{2,1,0:T(8,128)(2,1)S(1)}, bf16[2,16,2048]{2,1,0:T(8,128)(2,1)S(1)}, u32[]{:S(2)}, u32[]{:S(2)}) collective-permute-start(bf16[2,16,2048]{2,1,0:T(8,128)(2,1)S(1)} %get-tuple-element.36), channel_id=1, source_target_pairs={{0,96},{32,128},{64,160},{96,192},{128,224},{160,0},{192,32},{224,... | collective-permute-start | bytes 393224 | tf_op jit(solution)/shard_map/ppermute | solution.py:255
  32.6 2.8 %collective-permute-start.3 = (bf16[2,16,2048]{2,1,0:T(8,128)(2,1)S(1)}, bf16[2,16,2048]{2,1,0:T(8,128)(2,1)S(1)}, u32[]{:S(2)}, u32[]{:S(2)}) collective-permute-start(bf16[2,16,2048]{2,1,0:T(8,128)(2,1)S(1)} %get-tuple-element.37), channel_id=1, source_target_pairs={{0,160},{32,192},{64,224},{96,0},{128,32},{160,64},{192,96},{224,1... | collective-permute-start | bytes 393224 | tf_op jit(solution)/shard_map/ppermute | solution.py:255
  35.4 1.2 collective-permute-start.4
  36.6 2.4 %collective-permute-start.5 = (bf16[2,16,2048]{2,1,0:T(8,128)(2,1)S(1)}, bf16[2,16,2048]{2,1,0:T(8,128)(2,1)S(1)}, u32[]{:S(2)}, u32[]{:S(2)}) collective-permute-start(bf16[2,16,2048]{2,1,0:T(8,128)(2,1)S(1)} %get-tuple-element.39), channel_id=1, source_target_pairs={{0,192},{32,224},{64,0},{96,32},{128,64},{160,96},{192,128},{224,1... | collective-permute-start | bytes 393224 | tf_op jit(solution)/shard_map/ppermute | solution.py:255
  39.0 0.7 collective-permute-start.6
  39.7 7.2 %collective-permute-done.2.refs_1_ = bf16[2,16,2048]{2,1,0:T(8,128)(2,1)S(1)} collective-permute-done((bf16[2,16,2048]{2,1,0:T(8,128)(2,1)S(1)}, bf16[2,16,2048]{2,1,0:T(8,128)(2,1)S(1)}, u32[]{:S(2)}, u32[]{:S(2)}) %collective-permute-start.2) | collective-permute-done | bytes 131104 | tf_op jit(solution)/shard_map/ppermute | solution.py:255
  47.0 1.3 collective-permute-done.4.refs_3_
  48.2 3.3 %collective-permute-done.5.refs_4_ = bf16[2,16,2048]{2,1,0:T(8,128)(2,1)S(1)} collective-permute-done((bf16[2,16,2048]{2,1,0:T(8,128)(2,1)S(1)}, bf16[2,16,2048]{2,1,0:T(8,128)(2,1)S(1)}, u32[]{:S(2)}, u32[]{:S(2)}) %collective-permute-start.5) | collective-permute-done | bytes 131104 | tf_op jit(solution)/shard_map/ppermute | solution.py:255
  51.6 2.7 %collective-permute-done.6.refs_5_ = bf16[2,16,2048]{2,1,0:T(8,128)(2,1)S(1)} collective-permute-done((bf16[2,16,2048]{2,1,0:T(8,128)(2,1)S(1)}, bf16[2,16,2048]{2,1,0:T(8,128)(2,1)S(1)}, u32[]{:S(2)}, u32[]{:S(2)}) %collective-permute-start.6) | collective-permute-done | bytes 131104 | tf_op jit(solution)/shard_map/ppermute | solution.py:255
  54.3 0.7 collective-permute-done.7.refs_6_
  55.0 1.9 %route_pieces.1 = bf16[16,16,16,128]{3,2,1,0:T(8,128)(2,1)} custom-call(s32[2]{0:T(128)S(1)} %pad_add_fusion.place_ref, s32[16]{0:T(128)S(1)} %copy-done.5, s32[16]{0:T(128)S(1)} %copy-done.4, bf16[2,16,2048]{2,1,0:T(8,128)(2,1)S(1)} %collective-permute-done.1.refs_0_, bf16[2,16,2048]{2,1,0:T(8,128)(2,1)S(1)} %collective-permute-done.2.refs_1_, ...), custom_call_target="tpu_custom_call" | custom-call | bytes 2097152 | tf_op jit(solution)/shard_map/route_pieces/pallas_call | solution.py:84
  56.9 14.4 %all-to-all-start.1 = ((bf16[256,16,128]{2,1,0:T(8,128)(2,1)}), bf16[256,16,128]{2,1,0:T(8,128)(2,1)S(1)}, u32[]{:S(2)}, u32[]{:S(2)}) async-start(bf16[256,16,128]{2,1,0:T(8,128)(2,1)} %bitcast.8), calls=%async_computation.1 | async-start | bytes 2097152 | tf_op jit(solution)/shard_map/all_to_all | solution.py:249
  71.2 0.6 dynamic_slice.10
  73.8 0.6 dynamic_slice.11.live_ref
  74.4 11.6 %attend_own.1 = (bf16[16,3,192,128]{3,2,1,0:T(8,128)(2,1)S(1)}, f32[16,8,192]{2,1,0:T(8,128)S(1)}) custom-call(bf16[16,3,192,128]{3,2,1,0:T(8,128)(2,1)S(1)} %all-to-all-done.qkv_ref), custom_call_target="tpu_custom_call", output_to_operand_aliasing={{0}: (0, {})} | custom-call | flops 9663676416 | bytes 4718592 | tf_op jit(solution)/shard_map/attend_own/pallas_call | solution.py:162
  86.0 15.8 %all-to-all-done.1 = bf16[256,16,128]{2,1,0:T(8,128)(2,1)S(1)} async-done(((bf16[256,16,128]{2,1,0:T(8,128)(2,1)}), bf16[256,16,128]{2,1,0:T(8,128)(2,1)S(1)}, u32[]{:S(2)}, u32[]{:S(2)}) %all-to-all-start.1) | async-done | bytes 1048608 | tf_op jit(solution)/shard_map/all_to_all | solution.py:249
  101.8 9.7 %attend_ref.1 = bf16[16,192,128]{2,1,0:T(8,128)(2,1)S(1)} custom-call(s32[1]{0:T(128)} %dynamic_slice.11.live_ref, bf16[16,3,192,128]{3,2,1,0:T(8,128)(2,1)S(1)} %get-tuple-element.33.own_ref, f32[16,8,192]{2,1,0:T(8,128)S(1)} %get-tuple-element.34.stats_ref, bf16[8,2,16,16,128]{4,3,2,1,0:T(8,128)(2,1)S(1)} %bitcast.13), custom_call_target="tpu_custom_call" | custom-call | flops 6442450944 | bytes 6291456 | tf_op jit(solution)/shard_map/attend_ref/pallas_call | solution.py:230
  111.5 17.8 %all_to_all.15.x_ref = bf16[16,192,128]{2,1,0:T(8,128)(2,1)S(1)} all-to-all(bf16[16,192,128]{2,1,0:T(8,128)(2,1)S(1)} %attend_ref.1), channel_id=1, replica_groups=mesh['z'=8,'x'=2,'sp'=16] {'sp'}, dimensions={0} | all-to-all | bytes 1572864 | tf_op jit(solution)/shard_map/all_to_all | solution.py:249
  129.3 1.1 unpack_heads.1
  (13 shorter events, 0.0 us)
Async XLA Ops:
  1.1 14.3 %collective-permute-start = (bf16[128,2048]{1,0:T(8,128)(2,1)S(1)}, bf16[128,2048]{1,0:T(8,128)(2,1)S(1)}, u32[]{:S(2)}, u32[]{:S(2)}) collective-permute-start(bf16[128,2048]{1,0:T(8,128)(2,1)S(1)} %dynamic-slice_bitcast_fusion), channel_id=1, source_target_pairs={{0,16},{16,0},{1,17},{17,1},{2,18},{18,2},{3,19},{19,3},{4,20},{20... | collective-permute-start | bytes 1572872 | tf_op jit(solution)/shard_map/ppermute | solution.py:265
  4.7 1.1 copy-start.1
  5.9 1.1 copy-start.2
  7.0 1.1 copy-start.3
  8.1 7.2 %copy-start = (bf16[1,2,128,2048]{3,2,1,0:T(8,128)(2,1)S(1)}, bf16[1,2,128,2048]{3,2,1,0:T(8,128)(2,1)}, u32[]{:S(2)}) copy-start(bf16[1,2,128,2048]{3,2,1,0:T(8,128)(2,1)} %param.10) | copy-start | bytes 3145732
  16.0 39.0 %copy-start.4 = (s32[16]{0:T(128)S(1)}, s32[16]{0:T(128)}, u32[]{:S(2)}) copy-start(s32[16]{0:T(128)} %owner_ref.1) | copy-start | bytes 196
  16.0 39.0 %copy-start.5 = (s32[16]{0:T(128)S(1)}, s32[16]{0:T(128)}, u32[]{:S(2)}) copy-start(s32[16]{0:T(128)} %ids_ref.1) | copy-start | bytes 196
  16.0 40.9 %all-to-all-start = ((bf16[16,3,192,128]{3,2,1,0:T(8,128)(2,1)}), bf16[16,3,192,128]{3,2,1,0:T(8,128)(2,1)S(1)}, u32[]{:S(2)}, u32[]{:S(2)}) async-start(bf16[16,3,192,128]{3,2,1,0:T(8,128)(2,1)} %pack_heads.1), calls=%async_computation | async-start | bytes 4718592 | tf_op jit(solution)/shard_map/all_to_all | solution.py:249
  23.9 49.9 %copy-start.6 = (s32[16]{0:T(128)S(1)}, s32[16]{0:T(128)}, u32[]{:S(2)}) copy-start(s32[16]{0:T(128)} %param.13) | copy-start | bytes 196
  23.9 15.1 %collective-permute-start.1 = (bf16[2,16,2048]{2,1,0:T(8,128)(2,1)S(1)}, bf16[2,16,2048]{2,1,0:T(8,128)(2,1)S(1)}, u32[]{:S(2)}, u32[]{:S(2)}) collective-permute-start(bf16[2,16,2048]{2,1,0:T(8,128)(2,1)S(1)} %get-tuple-element.35), channel_id=1, source_target_pairs={{0,128},{32,160},{64,192},{96,224},{128,0},{160,32},{192,64},{224,... | collective-permute-start | bytes 393224 | tf_op jit(solution)/shard_map/ppermute | solution.py:255
  30.9 16.0 %collective-permute-start.2 = (bf16[2,16,2048]{2,1,0:T(8,128)(2,1)S(1)}, bf16[2,16,2048]{2,1,0:T(8,128)(2,1)S(1)}, u32[]{:S(2)}, u32[]{:S(2)}) collective-permute-start(bf16[2,16,2048]{2,1,0:T(8,128)(2,1)S(1)} %get-tuple-element.36), channel_id=1, source_target_pairs={{0,96},{32,128},{64,160},{96,192},{128,224},{160,0},{192,32},{224,... | collective-permute-start | bytes 393224 | tf_op jit(solution)/shard_map/ppermute | solution.py:255
  32.6 14.4 %collective-permute-start.3 = (bf16[2,16,2048]{2,1,0:T(8,128)(2,1)S(1)}, bf16[2,16,2048]{2,1,0:T(8,128)(2,1)S(1)}, u32[]{:S(2)}, u32[]{:S(2)}) collective-permute-start(bf16[2,16,2048]{2,1,0:T(8,128)(2,1)S(1)} %get-tuple-element.37), channel_id=1, source_target_pairs={{0,160},{32,192},{64,224},{96,0},{128,32},{160,64},{192,96},{224,1... | collective-permute-start | bytes 393224 | tf_op jit(solution)/shard_map/ppermute | solution.py:255
  35.4 12.8 %collective-permute-start.4 = (bf16[2,16,2048]{2,1,0:T(8,128)(2,1)S(1)}, bf16[2,16,2048]{2,1,0:T(8,128)(2,1)S(1)}, u32[]{:S(2)}, u32[]{:S(2)}) collective-permute-start(bf16[2,16,2048]{2,1,0:T(8,128)(2,1)S(1)} %get-tuple-element.38), channel_id=1, source_target_pairs={{0,64},{32,96},{64,128},{96,160},{128,192},{160,224},{192,0},{224,... | collective-permute-start | bytes 393224 | tf_op jit(solution)/shard_map/ppermute | solution.py:255
  36.6 15.0 %collective-permute-start.5 = (bf16[2,16,2048]{2,1,0:T(8,128)(2,1)S(1)}, bf16[2,16,2048]{2,1,0:T(8,128)(2,1)S(1)}, u32[]{:S(2)}, u32[]{:S(2)}) collective-permute-start(bf16[2,16,2048]{2,1,0:T(8,128)(2,1)S(1)} %get-tuple-element.39), channel_id=1, source_target_pairs={{0,192},{32,224},{64,0},{96,32},{128,64},{160,96},{192,128},{224,1... | collective-permute-start | bytes 393224 | tf_op jit(solution)/shard_map/ppermute | solution.py:255
  39.0 15.3 %collective-permute-start.6 = (bf16[2,16,2048]{2,1,0:T(8,128)(2,1)S(1)}, bf16[2,16,2048]{2,1,0:T(8,128)(2,1)S(1)}, u32[]{:S(2)}, u32[]{:S(2)}) collective-permute-start(bf16[2,16,2048]{2,1,0:T(8,128)(2,1)S(1)} %get-tuple-element.40), channel_id=1, source_target_pairs={{0,32},{32,64},{64,96},{96,128},{128,160},{160,192},{192,224},{224... | collective-permute-start | bytes 393224 | tf_op jit(solution)/shard_map/ppermute | solution.py:255
  47.0 8.0 %collective-permute-start.7 = (bf16[2,16,2048]{2,1,0:T(8,128)(2,1)S(1)}, bf16[2,16,2048]{2,1,0:T(8,128)(2,1)S(1)}, u32[]{:S(2)}, u32[]{:S(2)}) collective-permute-start(bf16[2,16,2048]{2,1,0:T(8,128)(2,1)S(1)} %get-tuple-element.41), channel_id=1, source_target_pairs={{0,224},{32,0},{64,32},{96,64},{128,96},{160,128},{192,160},{224,1... | collective-permute-start | bytes 393224 | tf_op jit(solution)/shard_map/ppermute | solution.py:255
  56.9 44.9 %all-to-all-start.1 = ((bf16[256,16,128]{2,1,0:T(8,128)(2,1)}), bf16[256,16,128]{2,1,0:T(8,128)(2,1)S(1)}, u32[]{:S(2)}, u32[]{:S(2)}) async-start(bf16[256,16,128]{2,1,0:T(8,128)(2,1)} %bitcast.8), calls=%async_computation.1 | async-start | bytes 2097152 | tf_op jit(solution)/shard_map/all_to_all | solution.py:249

commit v6 on v5

--- a/solution.py
+++ b/solution.py
@@ -95,9 +95,15 @@
     )(place, ids, owner, *pieces)
 
 
-def unpack_kernel(x_ref, out_ref):
+def unpack_kernel(x_ref, out_ref, sems):
+    def move(head):
+        columns = out_ref.at[:, head * D : (head + 1) * D]
+        return pltpu.make_async_copy(x_ref.at[head], columns, sems.at[head])
+
     for head in range(x_ref.shape[0]):
-        out_ref[:, head * D : (head + 1) * D] = x_ref[head]
+        move(head).start()
+    for head in range(x_ref.shape[0]):
+        move(head).wait()
 
 
 def unpack_heads(x):
@@ -105,8 +111,9 @@
     return pl.pallas_call(
         unpack_kernel,
         in_specs=[whole()],
-        out_specs=whole(),
+        out_specs=whole(pl.ANY),
         out_shape=jax.ShapeDtypeStruct((tokens, heads * D), x.dtype),
+        scratch_shapes=[pltpu.SemaphoreType.DMA((heads,))],
         compiler_params=params(),
         name="unpack_heads",
     )(x)

time: 131 us -> 131 us (level)
  no operation moved by 1% of the time
where the time goes in v6:
time: 131 us; the launch traced here: 130 us
  starting transfers between devices  41.8 us (32%)
  waiting for transfers between devices  36.3 us (28%)
  Pallas kernels  26.7 us (20%)
  blocking collectives  17.8 us (14%)
  local copies, waits for them, and re-layouts  5.67 us (4%)
  between operations  2.21 us (2%)
    all_to_all x2, starting transfers between devices, swap(): return lax.all_to_all(x, axes, split_axis=0, concat_axis=0, tiled=True)  22.3 us
    all_to_all x1, blocking collectives, swap(): return lax.all_to_all(x, axes, split_axis=0, concat_axis=0, tiled=True)  17.8 us
    all_to_all x2, waiting for transfers between devices, swap(): return lax.all_to_all(x, axes, split_axis=0, concat_axis=0, tiled=True)  15.8 us
    ppermute x7, starting transfers between devices, shift_z(): lax.ppermute(piece, 'z', [(src, (src + shift) % n_z) for src in range(n_z)])  15.8 us
    ppermute x7, waiting for transfers between devices, shift_z(): lax.ppermute(piece, 'z', [(src, (src + shift) % n_z) for src in range(n_z)])  15.2 us
    pallas_call x1, Pallas kernels, attend_own(): pl.pallas_call(functools.partial(own_kernel, per_row=PER_ROW, steps=4), g...  11.6 us
    pallas_call x1, Pallas kernels, attend_ref(): pl.pallas_call(functools.partial(ref_kernel, per_row=shards, steps=1), gr...  9.7 us
    ppermute x1, waiting for transfers between devices, shards(): other = lax.ppermute(other, 'x', [(0, 1), (1, 0)])  5.27 us
  transfers between devices with their start and end apart: 10, of which 7 were waited for; matrix products, arithmetic and copies ran while one was open for 1% of the time, Pallas kernels for 12%

profile of v6, /device:TPU:1, one launch (start us, length us, event | category | flops | bytes accessed | tf_op | source)
XLA Modules:
  0.0 130.5 jit_solution(7604915723004247987)
XLA Ops:
  0.0 1.1 dynamic-slice_bitcast_fusion
  1.1 3.7 %collective-permute-start = (bf16[128,2048]{1,0:T(8,128)(2,1)S(1)}, bf16[128,2048]{1,0:T(8,128)(2,1)S(1)}, u32[]{:S(2)}, u32[]{:S(2)}) collective-permute-start(bf16[128,2048]{1,0:T(8,128)(2,1)S(1)} %dynamic-slice_bitcast_fusion), channel_id=1, source_target_pairs={{0,16},{16,0},{1,17},{17,1},{2,18},{18,2},{3,19},{19,3},{4,20},{20... | collective-permute-start | bytes 1572872 | tf_op jit(solution)/shard_map/ppermute | solution.py:272
  4.7 1.1 copy-done.1
  5.9 1.1 copy-done.2
  7.0 1.1 copy-done.3
  8.1 1.8 %pack_heads.1 = bf16[16,3,192,128]{3,2,1,0:T(8,128)(2,1)} custom-call(bf16[192,2048]{1,0:T(8,128)(2,1)S(1)} %bitcast.14, bf16[192,2048]{1,0:T(8,128)(2,1)S(1)} %bitcast.15, bf16[192,2048]{1,0:T(8,128)(2,1)S(1)} %bitcast.16), custom_call_target="tpu_custom_call" | custom-call | bytes 4718592 | tf_op jit(solution)/shard_map/pack_heads/pallas_call | solution.py:36
  10.0 0.1 pad_add_fusion.place_ref
  10.1 5.3 %collective-permute-done.other_ref = bf16[128,2048]{1,0:T(8,128)(2,1)S(1)} collective-permute-done((bf16[128,2048]{1,0:T(8,128)(2,1)S(1)}, bf16[128,2048]{1,0:T(8,128)(2,1)S(1)}, u32[]{:S(2)}, u32[]{:S(2)}) %collective-permute-start) | collective-permute-done | bytes 524320 | tf_op jit(solution)/shard_map/ppermute | solution.py:272
  15.3 0.6 spread_pieces.1
  16.0 0.0 copy-start.4
  16.0 0.0 copy-start.5
  16.0 7.9 %all-to-all-start = ((bf16[16,3,192,128]{3,2,1,0:T(8,128)(2,1)}), bf16[16,3,192,128]{3,2,1,0:T(8,128)(2,1)S(1)}, u32[]{:S(2)}, u32[]{:S(2)}) async-start(bf16[16,3,192,128]{3,2,1,0:T(8,128)(2,1)} %pack_heads.1), calls=%async_computation | async-start | bytes 4718592 | tf_op jit(solution)/shard_map/all_to_all | solution.py:256
  23.9 7.0 %collective-permute-start.1 = (bf16[2,16,2048]{2,1,0:T(8,128)(2,1)S(1)}, bf16[2,16,2048]{2,1,0:T(8,128)(2,1)S(1)}, u32[]{:S(2)}, u32[]{:S(2)}) collective-permute-start(bf16[2,16,2048]{2,1,0:T(8,128)(2,1)S(1)} %get-tuple-element.35), channel_id=1, source_target_pairs={{0,128},{32,160},{64,192},{96,224},{128,0},{160,32},{192,64},{224,... | collective-permute-start | bytes 393224 | tf_op jit(solution)/shard_map/ppermute | solution.py:262
  30.9 1.6 %collective-permute-start.2 = (bf16[2,16,2048]{2,1,0:T(8,128)(2,1)S(1)}, bf16[2,16,2048]{2,1,0:T(8,128)(2,1)S(1)}, u32[]{:S(2)}, u32[]{:S(2)}) collective-permute-start(bf16[2,16,2048]{2,1,0:T(8,128)(2,1)S(1)} %get-tuple-element.36), channel_id=1, source_target_pairs={{0,96},{32,128},{64,160},{96,192},{128,224},{160,0},{192,32},{224,... | collective-permute-start | bytes 393224 | tf_op jit(solution)/shard_map/ppermute | solution.py:262
  32.6 2.8 %collective-permute-start.3 = (bf16[2,16,2048]{2,1,0:T(8,128)(2,1)S(1)}, bf16[2,16,2048]{2,1,0:T(8,128)(2,1)S(1)}, u32[]{:S(2)}, u32[]{:S(2)}) collective-permute-start(bf16[2,16,2048]{2,1,0:T(8,128)(2,1)S(1)} %get-tuple-element.37), channel_id=1, source_target_pairs={{0,160},{32,192},{64,224},{96,0},{128,32},{160,64},{192,96},{224,1... | collective-permute-start | bytes 393224 | tf_op jit(solution)/shard_map/ppermute | solution.py:262
  35.4 1.2 collective-permute-start.4
  36.6 2.4 %collective-permute-start.5 = (bf16[2,16,2048]{2,1,0:T(8,128)(2,1)S(1)}, bf16[2,16,2048]{2,1,0:T(8,128)(2,1)S(1)}, u32[]{:S(2)}, u32[]{:S(2)}) collective-permute-start(bf16[2,16,2048]{2,1,0:T(8,128)(2,1)S(1)} %get-tuple-element.39), channel_id=1, source_target_pairs={{0,192},{32,224},{64,0},{96,32},{128,64},{160,96},{192,128},{224,1... | collective-permute-start | bytes 393224 | tf_op jit(solution)/shard_map/ppermute | solution.py:262
  39.0 0.7 collective-permute-start.6
  39.7 7.2 %collective-permute-done.2.refs_1_ = bf16[2,16,2048]{2,1,0:T(8,128)(2,1)S(1)} collective-permute-done((bf16[2,16,2048]{2,1,0:T(8,128)(2,1)S(1)}, bf16[2,16,2048]{2,1,0:T(8,128)(2,1)S(1)}, u32[]{:S(2)}, u32[]{:S(2)}) %collective-permute-start.2) | collective-permute-done | bytes 131104 | tf_op jit(solution)/shard_map/ppermute | solution.py:262
  47.0 1.3 collective-permute-done.4.refs_3_
  48.2 3.3 %collective-permute-done.5.refs_4_ = bf16[2,16,2048]{2,1,0:T(8,128)(2,1)S(1)} collective-permute-done((bf16[2,16,2048]{2,1,0:T(8,128)(2,1)S(1)}, bf16[2,16,2048]{2,1,0:T(8,128)(2,1)S(1)}, u32[]{:S(2)}, u32[]{:S(2)}) %collective-permute-start.5) | collective-permute-done | bytes 131104 | tf_op jit(solution)/shard_map/ppermute | solution.py:262
  51.6 2.7 %collective-permute-done.6.refs_5_ = bf16[2,16,2048]{2,1,0:T(8,128)(2,1)S(1)} collective-permute-done((bf16[2,16,2048]{2,1,0:T(8,128)(2,1)S(1)}, bf16[2,16,2048]{2,1,0:T(8,128)(2,1)S(1)}, u32[]{:S(2)}, u32[]{:S(2)}) %collective-permute-start.6) | collective-permute-done | bytes 131104 | tf_op jit(solution)/shard_map/ppermute | solution.py:262
  54.3 0.7 collective-permute-done.7.refs_6_
  55.0 1.9 %route_pieces.1 = bf16[16,16,16,128]{3,2,1,0:T(8,128)(2,1)} custom-call(s32[2]{0:T(128)S(1)} %pad_add_fusion.place_ref, s32[16]{0:T(128)S(1)} %copy-done.5, s32[16]{0:T(128)S(1)} %copy-done.4, bf16[2,16,2048]{2,1,0:T(8,128)(2,1)S(1)} %collective-permute-done.1.refs_0_, bf16[2,16,2048]{2,1,0:T(8,128)(2,1)S(1)} %collective-permute-done.2.refs_1_, ...), custom_call_target="tpu_custom_call" | custom-call | bytes 2097152 | tf_op jit(solution)/shard_map/route_pieces/pallas_call | solution.py:84
  56.9 14.4 %all-to-all-start.1 = ((bf16[256,16,128]{2,1,0:T(8,128)(2,1)}), bf16[256,16,128]{2,1,0:T(8,128)(2,1)S(1)}, u32[]{:S(2)}, u32[]{:S(2)}) async-start(bf16[256,16,128]{2,1,0:T(8,128)(2,1)} %bitcast.8), calls=%async_computation.1 | async-start | bytes 2097152 | tf_op jit(solution)/shard_map/all_to_all | solution.py:256
  71.2 0.6 dynamic_slice.10
  73.8 0.6 dynamic_slice.11.live_ref
  74.4 11.6 %attend_own.1 = (bf16[16,3,192,128]{3,2,1,0:T(8,128)(2,1)S(1)}, f32[16,8,192]{2,1,0:T(8,128)S(1)}) custom-call(bf16[16,3,192,128]{3,2,1,0:T(8,128)(2,1)S(1)} %all-to-all-done.qkv_ref), custom_call_target="tpu_custom_call", output_to_operand_aliasing={{0}: (0, {})} | custom-call | flops 9663676416 | bytes 4718592 | tf_op jit(solution)/shard_map/attend_own/pallas_call | solution.py:169
  86.0 15.8 %all-to-all-done.1 = bf16[256,16,128]{2,1,0:T(8,128)(2,1)S(1)} async-done(((bf16[256,16,128]{2,1,0:T(8,128)(2,1)}), bf16[256,16,128]{2,1,0:T(8,128)(2,1)S(1)}, u32[]{:S(2)}, u32[]{:S(2)}) %all-to-all-start.1) | async-done | bytes 1048608 | tf_op jit(solution)/shard_map/all_to_all | solution.py:256
  101.8 9.7 %attend_ref.1 = bf16[16,192,128]{2,1,0:T(8,128)(2,1)S(1)} custom-call(s32[1]{0:T(128)} %dynamic_slice.11.live_ref, bf16[16,3,192,128]{3,2,1,0:T(8,128)(2,1)S(1)} %get-tuple-element.33.own_ref, f32[16,8,192]{2,1,0:T(8,128)S(1)} %get-tuple-element.34.stats_ref, bf16[8,2,16,16,128]{4,3,2,1,0:T(8,128)(2,1)S(1)} %bitcast.13), custom_call_target="tpu_custom_call" | custom-call | flops 6442450944 | bytes 6291456 | tf_op jit(solution)/shard_map/attend_ref/pallas_call | solution.py:237
  111.5 17.8 %all_to_all.15.x_ref = bf16[16,192,128]{2,1,0:T(8,128)(2,1)S(1)} all-to-all(bf16[16,192,128]{2,1,0:T(8,128)(2,1)S(1)} %attend_ref.1), channel_id=1, replica_groups=mesh['z'=8,'x'=2,'sp'=16] {'sp'}, dimensions={0} | all-to-all | bytes 1572864 | tf_op jit(solution)/shard_map/all_to_all | solution.py:256
  129.3 1.0 unpack_heads.1
  (13 shorter events, 0.0 us)
Async XLA Ops:
  1.1 14.3 %collective-permute-start = (bf16[128,2048]{1,0:T(8,128)(2,1)S(1)}, bf16[128,2048]{1,0:T(8,128)(2,1)S(1)}, u32[]{:S(2)}, u32[]{:S(2)}) collective-permute-start(bf16[128,2048]{1,0:T(8,128)(2,1)S(1)} %dynamic-slice_bitcast_fusion), channel_id=1, source_target_pairs={{0,16},{16,0},{1,17},{17,1},{2,18},{18,2},{3,19},{19,3},{4,20},{20... | collective-permute-start | bytes 1572872 | tf_op jit(solution)/shard_map/ppermute | solution.py:272
  4.7 1.1 copy-start.1
  5.9 1.1 copy-start.2
  7.0 1.1 copy-start.3
  8.1 7.2 %copy-start = (bf16[1,2,128,2048]{3,2,1,0:T(8,128)(2,1)S(1)}, bf16[1,2,128,2048]{3,2,1,0:T(8,128)(2,1)}, u32[]{:S(2)}) copy-start(bf16[1,2,128,2048]{3,2,1,0:T(8,128)(2,1)} %param.10) | copy-start | bytes 3145732
  16.0 39.0 %copy-start.4 = (s32[16]{0:T(128)S(1)}, s32[16]{0:T(128)}, u32[]{:S(2)}) copy-start(s32[16]{0:T(128)} %owner_ref.1) | copy-start | bytes 196
  16.0 39.0 %copy-start.5 = (s32[16]{0:T(128)S(1)}, s32[16]{0:T(128)}, u32[]{:S(2)}) copy-start(s32[16]{0:T(128)} %ids_ref.1) | copy-start | bytes 196
  16.0 40.9 %all-to-all-start = ((bf16[16,3,192,128]{3,2,1,0:T(8,128)(2,1)}), bf16[16,3,192,128]{3,2,1,0:T(8,128)(2,1)S(1)}, u32[]{:S(2)}, u32[]{:S(2)}) async-start(bf16[16,3,192,128]{3,2,1,0:T(8,128)(2,1)} %pack_heads.1), calls=%async_computation | async-start | bytes 4718592 | tf_op jit(solution)/shard_map/all_to_all | solution.py:256
  23.9 49.9 %copy-start.6 = (s32[16]{0:T(128)S(1)}, s32[16]{0:T(128)}, u32[]{:S(2)}) copy-start(s32[16]{0:T(128)} %param.13) | copy-start | bytes 196
  23.9 15.1 %collective-permute-start.1 = (bf16[2,16,2048]{2,1,0:T(8,128)(2,1)S(1)}, bf16[2,16,2048]{2,1,0:T(8,128)(2,1)S(1)}, u32[]{:S(2)}, u32[]{:S(2)}) collective-permute-start(bf16[2,16,2048]{2,1,0:T(8,128)(2,1)S(1)} %get-tuple-element.35), channel_id=1, source_target_pairs={{0,128},{32,160},{64,192},{96,224},{128,0},{160,32},{192,64},{224,... | collective-permute-start | bytes 393224 | tf_op jit(solution)/shard_map/ppermute | solution.py:262
  30.9 16.0 %collective-permute-start.2 = (bf16[2,16,2048]{2,1,0:T(8,128)(2,1)S(1)}, bf16[2,16,2048]{2,1,0:T(8,128)(2,1)S(1)}, u32[]{:S(2)}, u32[]{:S(2)}) collective-permute-start(bf16[2,16,2048]{2,1,0:T(8,128)(2,1)S(1)} %get-tuple-element.36), channel_id=1, source_target_pairs={{0,96},{32,128},{64,160},{96,192},{128,224},{160,0},{192,32},{224,... | collective-permute-start | bytes 393224 | tf_op jit(solution)/shard_map/ppermute | solution.py:262
  32.6 14.4 %collective-permute-start.3 = (bf16[2,16,2048]{2,1,0:T(8,128)(2,1)S(1)}, bf16[2,16,2048]{2,1,0:T(8,128)(2,1)S(1)}, u32[]{:S(2)}, u32[]{:S(2)}) collective-permute-start(bf16[2,16,2048]{2,1,0:T(8,128)(2,1)S(1)} %get-tuple-element.37), channel_id=1, source_target_pairs={{0,160},{32,192},{64,224},{96,0},{128,32},{160,64},{192,96},{224,1... | collective-permute-start | bytes 393224 | tf_op jit(solution)/shard_map/ppermute | solution.py:262
  35.4 12.8 %collective-permute-start.4 = (bf16[2,16,2048]{2,1,0:T(8,128)(2,1)S(1)}, bf16[2,16,2048]{2,1,0:T(8,128)(2,1)S(1)}, u32[]{:S(2)}, u32[]{:S(2)}) collective-permute-start(bf16[2,16,2048]{2,1,0:T(8,128)(2,1)S(1)} %get-tuple-element.38), channel_id=1, source_target_pairs={{0,64},{32,96},{64,128},{96,160},{128,192},{160,224},{192,0},{224,... | collective-permute-start | bytes 393224 | tf_op jit(solution)/shard_map/ppermute | solution.py:262
  36.6 15.0 %collective-permute-start.5 = (bf16[2,16,2048]{2,1,0:T(8,128)(2,1)S(1)}, bf16[2,16,2048]{2,1,0:T(8,128)(2,1)S(1)}, u32[]{:S(2)}, u32[]{:S(2)}) collective-permute-start(bf16[2,16,2048]{2,1,0:T(8,128)(2,1)S(1)} %get-tuple-element.39), channel_id=1, source_target_pairs={{0,192},{32,224},{64,0},{96,32},{128,64},{160,96},{192,128},{224,1... | collective-permute-start | bytes 393224 | tf_op jit(solution)/shard_map/ppermute | solution.py:262
  39.0 15.3 %collective-permute-start.6 = (bf16[2,16,2048]{2,1,0:T(8,128)(2,1)S(1)}, bf16[2,16,2048]{2,1,0:T(8,128)(2,1)S(1)}, u32[]{:S(2)}, u32[]{:S(2)}) collective-permute-start(bf16[2,16,2048]{2,1,0:T(8,128)(2,1)S(1)} %get-tuple-element.40), channel_id=1, source_target_pairs={{0,32},{32,64},{64,96},{96,128},{128,160},{160,192},{192,224},{224... | collective-permute-start | bytes 393224 | tf_op jit(solution)/shard_map/ppermute | solution.py:262
  47.0 8.0 %collective-permute-start.7 = (bf16[2,16,2048]{2,1,0:T(8,128)(2,1)S(1)}, bf16[2,16,2048]{2,1,0:T(8,128)(2,1)S(1)}, u32[]{:S(2)}, u32[]{:S(2)}) collective-permute-start(bf16[2,16,2048]{2,1,0:T(8,128)(2,1)S(1)} %get-tuple-element.41), channel_id=1, source_target_pairs={{0,224},{32,0},{64,32},{96,64},{128,96},{160,128},{192,160},{224,1... | collective-permute-start | bytes 393224 | tf_op jit(solution)/shard_map/ppermute | solution.py:262
  56.9 44.9 %all-to-all-start.1 = ((bf16[256,16,128]{2,1,0:T(8,128)(2,1)}), bf16[256,16,128]{2,1,0:T(8,128)(2,1)S(1)}, u32[]{:S(2)}, u32[]{:S(2)}) async-start(bf16[256,16,128]{2,1,0:T(8,128)(2,1)} %bitcast.8), calls=%async_computation.1 | async-start | bytes 2097152 | tf_op jit(solution)/shard_map/all_to_all | solution.py:256
